TPU v7x, 256 devices: a whole 4x4x8 slice. The times are simulated.
256 devices in a mesh: dp: 8 (over y, z_hi), seq: 4 (over x), tensor: 8 (over z_lo, core).
Axes of the slice: x: 4, y: 4, z: 8 (z_hi: 2, z_lo: 4; z = z_hi * 4 + z_lo), core: 2. Of those that a mesh axis runs over, the one named last changes fastest.
Arguments:
- rows: bfloat16 [8, 512, 4096], P('dp', 'seq', 'tensor'), may hold values from -6 to 6
- keys: bfloat16 [8, 1024, 4096], P('dp', 'seq', 'tensor'), may hold values from -6 to 6
- values: bfloat16 [8, 1024, 4096], P('dp', 'seq', 'tensor'), may hold values from -18 to 18
- target_ids: int32 [8, 512], P('dp', 'seq'), may hold values from 0 to 3, as said below
- source_ids: int32 [8, 1024], P('dp'), may hold values from 0 to 3, as said below
- row_counts: int32 [8, 4], P('dp'), may hold values from 32 to 128, as said below
- w_query: bfloat16 [4096, 4096], P(None, 'tensor'), may hold values from -0.09375 to 0.09375
- w_output: bfloat16 [4096, 4096], P('tensor'), may hold values from -0.09375 to 0.09375
- query_gain: float32 [4096], P('tensor'), may hold values from 0.3 to 2.5
- key_gain: float32 [4096], P('tensor'), may hold values from 0.3 to 2.5
- cotangent: bfloat16 [8, 512, 4096], P('dp', 'seq', 'tensor'), may hold values from -6 to 6
Outputs:
- branch: bfloat16 [8, 512, 4096], P('dp', 'seq', 'tensor')
- rows_grad: bfloat16 [8, 512, 4096], P('dp', 'seq', 'tensor')
- keys_grad: bfloat16 [8, 1024, 4096], P('dp', 'seq', 'tensor')
- values_grad: bfloat16 [8, 1024, 4096], P('dp', 'seq', 'tensor')
- query_weight_grad: float32 [4096, 4096], P(('dp', 'seq'), 'tensor')
- output_weight_grad: float32 [4096, 4096], P('tensor', ('dp', 'seq'))
Inputs may be any that keep to these rules, and one draw needn't show every extreme that they name: `target_ids`: within a batch the ids never fall; every id from 0 to 3 labels one or more target slots. `source_ids`: within a batch the ids never fall; every id from 0 to 3 labels one or more encoder tokens. `row_counts`: in every batch some block is full.
All inputs are finite; a program needn't handle non-finite values.
Results may differ from a plain program's by a relative error of at most 0.03.
The roundings to bfloat16 on the way count: a program that leaves them out, or rounds other values in their place, can miss the bound.
Values may be sent and summed in bfloat16 or wider, within the bound.
No kernel may reach another device: no remote copies, remote signals or barrier semaphores. Data moves between devices by JAX's collectives and lax.ppermute only.
A program may use at most 128 MiB of HBM per device.

v0:
```python
import jax
import jax.numpy as jnp
from jax import lax
from jax.sharding import PartitionSpec as P

HS = 64


EPS = 1e-06


def norm_fwd(tensor, gain):
    average = jnp.mean(tensor, axis=-1, keepdims=True)
    centred = tensor - average
    variance = jnp.mean(centred * centred, axis=-1, keepdims=True)
    inverse = lax.rsqrt(variance + EPS)
    normed = centred * inverse
    return (normed, inverse, normed * gain)


def norm_bwd(upstream, normed, inverse, gain):
    scaled = upstream * gain
    return inverse * (
        scaled
        - jnp.mean(scaled, axis=-1, keepdims=True)
        - normed * jnp.mean(scaled * normed, axis=-1, keepdims=True)
    )


def head_work(inputs, allowed, livef):
    q_head, k_head, v_head, g_head = inputs
    contract = (((1,), (1,)), ((), ()))
    inner = (((0,), (0,)), ((), ()))
    scores = lax.dot_general(q_head, k_head, contract, preferred_element_type=jnp.float32)
    scores = jnp.where(allowed, scores, -jnp.inf)
    highest = jnp.max(scores, axis=-1, keepdims=True)
    expo = jnp.exp(scores - highest)
    probs = expo / jnp.sum(expo, axis=-1, keepdims=True) * livef[:, None]
    plow = probs.astype(jnp.bfloat16)
    attended = jnp.dot(plow, v_head, preferred_element_type=jnp.float32).astype(jnp.bfloat16)
    delta = jnp.sum(g_head.astype(jnp.float32) * attended.astype(jnp.float32), axis=-1)
    dprobs = lax.dot_general(g_head, v_head, contract, preferred_element_type=jnp.float32)
    sgrad = (probs * (dprobs - delta[:, None])).astype(jnp.bfloat16)
    qn_grad = jnp.dot(sgrad, k_head, preferred_element_type=jnp.float32)
    kn_part = lax.dot_general(sgrad, q_head, inner, preferred_element_type=jnp.float32)
    v_part = lax.dot_general(plow, g_head, inner, preferred_element_type=jnp.float32)
    return (attended, qn_grad, kn_part, v_part)


def body(
    rows,
    keys,
    values,
    target_ids,
    source_ids,
    row_counts,
    w_query,
    w_output,
    query_gain,
    key_gain,
    cotangent,
):
    local_width = w_query.shape[1]
    heads = local_width // HS
    tgt_rows = rows.shape[1]
    own_rows = keys.shape[1]
    qgain = query_gain.reshape(heads, HS)
    kgain = key_gain.reshape(heads, HS)
    seq_place = lax.axis_index("seq")
    blocks = jnp.arange(lax.axis_size("seq"), dtype=jnp.int32)
    live_count = jnp.sum(jnp.where(blocks == seq_place, row_counts[0], 0))
    livef = (jnp.arange(tgt_rows, dtype=jnp.int32) < live_count).astype(jnp.float32)
    states_all, cot_all = (
        lax.all_gather(rows, "tensor", axis=2, tiled=True),
        lax.all_gather(cotangent, "tensor", axis=2, tiled=True),
    )
    states = states_all[0]
    cot_full = cot_all[0]
    query = jnp.dot(states, w_query, preferred_element_type=jnp.float32)
    qhat, qinverse, qnormed = norm_fwd(query.reshape(tgt_rows, heads, HS), qgain)
    query_reduced_precision = qnormed.astype(jnp.bfloat16)
    keys_all, values_all = (
        lax.all_gather(keys, "seq", axis=1, tiled=True),
        lax.all_gather(values, "seq", axis=1, tiled=True),
    )
    khat_all, kinv_all, every_key_normed = norm_fwd(
        keys_all[0].astype(jnp.float32).reshape(-1, heads, HS), kgain
    )
    key_reduced_precision = every_key_normed.astype(jnp.bfloat16)
    offset = seq_place * own_rows
    khat = lax.dynamic_slice_in_dim(khat_all, offset, own_rows, 0)
    kinverse = lax.dynamic_slice_in_dim(kinv_all, offset, own_rows, 0)
    gathered_values = values_all[0]
    value_rows = gathered_values.reshape(-1, heads, HS)
    allowed = target_ids[0][:, None] == source_ids[0][None, :]
    att_grad = lax.dot_general(
        cot_full, w_output, (((1,), (1,)), ((), ())), preferred_element_type=jnp.float32
    ).astype(jnp.bfloat16)
    gradient_triple3 = att_grad.reshape(tgt_rows, heads, HS)

    def head_wise(head_inputs):
        return head_work(head_inputs, allowed, livef)

    head_attention, head_query_normed, head_key_normed, head_value_gradient = lax.map(
        head_wise,
        (
            jnp.transpose(query_reduced_precision, (1, 0, 2)),
            jnp.transpose(key_reduced_precision, (1, 0, 2)),
            jnp.transpose(value_rows, (1, 0, 2)),
            jnp.transpose(gradient_triple3, (1, 0, 2)),
        ),
    )
    attended = jnp.transpose(head_attention, (1, 0, 2))
    qn_grad = jnp.transpose(head_query_normed, (1, 0, 2))
    flat = attended.reshape(tgt_rows, local_width)
    out_part = jnp.dot(flat, w_output, preferred_element_type=jnp.float32)
    branch = lax.psum_scatter(
        out_part[None].astype(jnp.bfloat16), "tensor", scatter_dimension=2, tiled=True
    )
    query_grad = (
        norm_bwd(qn_grad, qhat, qinverse, qgain).reshape(tgt_rows, local_width).astype(jnp.bfloat16)
    )
    kn_part = jnp.transpose(head_key_normed, (1, 0, 2)).reshape(1, -1, local_width)
    v_part = jnp.transpose(head_value_gradient, (1, 0, 2)).reshape(1, -1, local_width)
    kn_sum, v_sum = (
        lax.psum_scatter(
            kn_part.astype(jnp.bfloat16), "seq", scatter_dimension=1, tiled=True
        ).astype(jnp.float32),
        lax.psum_scatter(
            v_part.astype(jnp.bfloat16), "seq", scatter_dimension=1, tiled=True
        ).astype(jnp.float32),
    )
    keys_grad = norm_bwd(kn_sum[0].reshape(own_rows, heads, HS), khat, kinverse, kgain)
    keys_grad = keys_grad.reshape(1, own_rows, local_width).astype(jnp.bfloat16)
    values_grad = v_sum.astype(jnp.bfloat16)
    x_part = lax.dot_general(
        query_grad, w_query, (((1,), (1,)), ((), ())), preferred_element_type=jnp.float32
    )
    rows_grad = lax.psum_scatter(
        x_part[None].astype(jnp.bfloat16), "tensor", scatter_dimension=2, tiled=True
    )
    columns = states
    query_weight_grad = lax.psum_scatter(
        lax.dot_general(
            columns, query_grad, (((0,), (0,)), ((), ())), preferred_element_type=jnp.float32
        ).astype(jnp.bfloat16),
        ("dp", "seq"),
        scatter_dimension=0,
        tiled=True,
    ).astype(jnp.float32)
    columns = cot_full
    output_weight_grad = (
        lax.psum_scatter(
            lax.dot_general(
                columns, flat, (((0,), (0,)), ((), ())), preferred_element_type=jnp.float32
            ).astype(jnp.bfloat16),
            ("dp", "seq"),
            scatter_dimension=0,
            tiled=True,
        )
        .astype(jnp.float32)
        .T
    )
    return (branch, rows_grad, keys_grad, values_grad, query_weight_grad, output_weight_grad)


def solution(mesh):
    in_specs = (
        P("dp", "seq", "tensor"),
        P("dp", "seq", "tensor"),
        P("dp", "seq", "tensor"),
        P("dp", "seq"),
        P("dp", None),
        P("dp", None),
        P(None, "tensor"),
        P("tensor", None),
        P("tensor"),
        P("tensor"),
        P("dp", "seq", "tensor"),
    )
    out_specs = (
        P("dp", "seq", "tensor"),
        P("dp", "seq", "tensor"),
        P("dp", "seq", "tensor"),
        P("dp", "seq", "tensor"),
        P(("dp", "seq"), "tensor"),
        P("tensor", ("dp", "seq")),
    )
    return jax.shard_map(body, mesh=mesh, in_specs=in_specs, out_specs=out_specs, check_vma=False)
```

profile of v0, /device:TPU:32, one launch (start us, length us, event | category | flops | bytes accessed | tf_op | source)
XLA Modules:
  0.0 825.1 jit_solution(10401504537815513006)
XLA Ops:
  7.2 1.8 copy.34
  10.6 1.8 copy.35
  12.5 6.4 copy.33
  19.7 21.7 %all-gather.7.cloned.1.call-done = bf16[1,1024,512]{1,2,0:T(8,128)(2,1)} async-done(((bf16[1,256,512]{1,2,0:T(8,128)(2,1)}), bf16[1,1024,512]{1,2,0:T(8,128)(2,1)}) %all-gather.7.cloned.1.call-update) | async-done | bytes 1048592 | tf_op jit(solution)/shard_map/all_gather | solution.py:83
  42.9 1.6 fusion.40
  45.1 1.6 fusion.38
  46.7 31.7 %all-gather.11.cloned.1.call-done = bf16[1,128,4096]{2,1,0:T(8,128)(2,1)} async-done(((bf16[1,128,512]{2,1,0:T(8,128)(2,1)}), bf16[1,128,4096]{2,1,0:T(8,128)(2,1)}) %all-gather.11.cloned.1.call-update) | async-done | bytes 1048592 | tf_op jit(solution)/shard_map/all_gather | solution.py:75
  78.4 4.0 convolution_convert_fusion.5
  83.2 33.1 %all-gather.5.cloned.1.call-done = bf16[1,128,4096]{2,1,0:T(8,128)(2,1)} async-done(((bf16[1,128,512]{2,1,0:T(8,128)(2,1)}), bf16[1,128,4096]{2,1,0:T(8,128)(2,1)}) %all-gather.5.cloned.1.call-update) | async-done | bytes 1048592 | tf_op jit(solution)/shard_map/all_gather | solution.py:74
  116.3 3.8 fusion.65
  121.5 27.4 %all-gather.9.cloned.1.call-done = bf16[1,1024,512]{1,2,0:T(8,128)(2,1)} async-done(((bf16[1,256,512]{1,2,0:T(8,128)(2,1)}), bf16[1,1024,512]{1,2,0:T(8,128)(2,1)}) %all-gather.9.cloned.1.call-update) | async-done | bytes 1048592 | tf_op jit(solution)/shard_map/all_gather | solution.py:84
  148.8 73.2 %while.17 = (s32[]{:T(128)}, bf16[8,128,64]{1,2,0:T(8,128)(2,1)S(1)}, f32[8,128,64]{1,2,0:T(8,128)}, bf16[8,1024,64]{1,2,0:T(8,128)(2,1)}, bf16[8,1024,64]{1,2,0...) while((s32[]{:T(128)}, ...), condition=%wide.region_9.10_spmd.clone, body=%wide.region_5.9_spmd.clone.sunk | while | flops 103194496 | bytes 4638861 | solution.py:104
  156.3 1.7 fusion.103
  165.5 1.7 fusion.103
  174.6 1.7 fusion.103
  183.7 1.7 fusion.103
  192.9 1.7 fusion.103
  202.0 1.7 fusion.103
  211.2 1.7 fusion.103
  220.3 1.7 fusion.103
  224.9 4.4 fusion.34
  229.3 6.5 copy.43
  237.0 3.2 fusion.35
  240.3 6.6 copy.45
  246.9 4.1 fusion.36
  251.0 4.7 fusion.37
  259.6 18.2 %reduce-scatter.17.cloned.1.call-done = bf16[1,256,512]{1,2,0:T(8,128)(2,1)} async-done(((bf16[1,1024,512]{1,2,0:T(8,128)(2,1)}), bf16[1,256,512]{1,2,0:T(8,128)(2,1)}) %reduce-scatter.17.cloned.1.call-update) | async-done | bytes 262160 | tf_op jit(solution)/shard_map/reduce_scatter | solution.py:129
  277.7 1.8 copy.41
  279.5 236.8 %reduce-scatter.19.cloned.1.call-done = bf16[128,512]{1,0:T(8,128)(2,1)} async-done(((bf16[4096,512]{1,0:T(8,128)(2,1)}), bf16[128,512]{1,0:T(8,128)(2,1)}) %reduce-scatter.19.cloned.1.call-update) | async-done | bytes 131088
  518.2 230.6 %reduce-scatter.21.cloned.1.call-done = bf16[128,512]{1,0:T(8,128)(2,1)} async-done(((bf16[4096,512]{1,0:T(8,128)(2,1)}), bf16[128,512]{1,0:T(8,128)(2,1)}) %reduce-scatter.21.cloned.1.call-update) | async-done | bytes 131088
  750.5 28.1 %reduce-scatter.11.cloned.1.call-done = bf16[1,128,512]{2,1,0:T(8,128)(2,1)} async-done(((bf16[1,128,4096]{2,1,0:T(8,128)(2,1)}), bf16[1,128,512]{2,1,0:T(8,128)(2,1)}) %reduce-scatter.11.cloned.1.call-update) | async-done | bytes 131088 | tf_op jit(solution)/shard_map/reduce_scatter | solution.py:117
  778.6 39.6 %reduce-scatter.13.cloned.1.call-done = bf16[1,128,512]{2,1,0:T(8,128)(2,1)} async-done(((bf16[1,128,4096]{2,1,0:T(8,128)(2,1)}), bf16[1,128,512]{2,1,0:T(8,128)(2,1)}) %reduce-scatter.13.cloned.1.call-update) | async-done | bytes 131088 | tf_op jit(solution)/shard_map/reduce_scatter | solution.py:139
  (124 shorter events, 77.8 us)
Async XLA Ops:
  7.2 34.2 %all-gather.7.cloned.1.call-start = ((), (), s32[]{:S(2)}) async-start(), calls=%async_computation.7 | async-start | bytes 1310720 | tf_op jit(solution)/shard_map/all_gather | solution.py:83
  9.0 69.3 %all-gather.11.cloned.1.call-start = ((), (), s32[]{:S(2)}) async-start(), calls=%async_computation.9 | async-start | bytes 1179648 | tf_op jit(solution)/shard_map/all_gather | solution.py:75
  9.8 106.5 %all-gather.5.cloned.1.call-start = ((), (), s32[]{:S(2)}) async-start(), calls=%async_computation.6 | async-start | bytes 1179648 | tf_op jit(solution)/shard_map/all_gather | solution.py:74
  10.5 138.3 %all-gather.9.cloned.1.call-start = ((), (), s32[]{:S(2)}) async-start(), calls=%async_computation.8 | async-start | bytes 1310720 | tf_op jit(solution)/shard_map/all_gather | solution.py:84
  12.4 244.0 %reduce-scatter.15.cloned.1.call-start = ((), (), s32[]{:S(2)}) async-start(), calls=%async_computation.12 | async-start | bytes 1310720 | tf_op jit(solution)/shard_map/reduce_scatter | solution.py:126
  12.5 6.5 copy-start.3
  12.5 6.5 copy-start.4
  12.5 6.6 copy-start.5
  44.4 0.6 copy-start.1
  82.4 66.4 %copy-start.2 = (s32[1,1024]{1,0:T(1,128)S(1)}, s32[1,1024]{1,0:T(1,128)}, u32[]{:S(2)}) copy-start(s32[1,1024]{1,0:T(1,128)} %param.17) | copy-start | bytes 12292
  222.1 55.7 %reduce-scatter.17.cloned.1.call-start = ((), (), s32[]{:S(2)}) async-start(), calls=%async_computation.13 | async-start | bytes 1310720 | tf_op jit(solution)/shard_map/reduce_scatter | solution.py:129
  222.6 293.7 %reduce-scatter.19.cloned.1.call-start = ((), (), s32[]{:S(2)}) async-start(), calls=%async_computation.14 | async-start | bytes 4325376
  235.8 1.2 copy-start
  235.8 512.9 %reduce-scatter.21.cloned.1.call-start = ((), (), s32[]{:S(2)}) async-start(), calls=%async_computation.15 | async-start | bytes 4325376
  246.8 531.8 %reduce-scatter.11.cloned.1.call-start = ((), (), s32[]{:S(2)}) async-start(), calls=%async_computation.10 | async-start | bytes 1179648 | tf_op jit(solution)/shard_map/reduce_scatter | solution.py:117
  251.0 567.2 %reduce-scatter.13.cloned.1.call-start = ((), (), s32[]{:S(2)}) async-start(), calls=%async_computation.11 | async-start | bytes 1179648 | tf_op jit(solution)/shard_map/reduce_scatter | solution.py:139
Sparse Core Ops, SparseCore 0:
  10.4 30.9 all-gather.6
  43.2 35.1 all-gather.10
  80.2 36.0 all-gather.4
  118.5 30.2 all-gather.8
  222.2 27.0 reduce-scatter.14
  251.9 25.8 reduce-scatter.16
  280.2 236.0 reduce-scatter.18
  518.8 229.8 reduce-scatter.20
  751.9 26.7 reduce-scatter.10
  781.6 36.5 reduce-scatter.12
where the time goes:
time: 833 us; the launch traced here: 825 us
  waiting for transfers between devices  669 us (80%)
  matrix products  84.5 us (10%)
  local copies, waits for them, and re-layouts  31.9 us (4%)
  other arithmetic  24.7 us (3%)
  between operations  14.4 us (2%)
    unnamed x12, waiting for transfers between devices  469 us
    reduce_scatter x1, waiting for transfers between devices, body(): lax.psum_scatter(x_part[None].astype(jnp.bfloat16), 'tensor', scatter_dim...  39.6 us
    all_gather x1, waiting for transfers between devices, body(): lax.all_gather(rows, 'tensor', axis=2, tiled=True)  33.1 us
    all_gather x1, waiting for transfers between devices, body(): lax.all_gather(cotangent, 'tensor', axis=2, tiled=True)  31.7 us
    unnamed x22, local copies, waits for them, and re-layouts  30.3 us
    reduce_scatter x1, waiting for transfers between devices, body(): lax.psum_scatter(out_part[None].astype(jnp.bfloat16), 'tensor', scatter_d...  28.1 us
    all_gather x1, waiting for transfers between devices, body(): lax.all_gather(values, 'seq', axis=1, tiled=True)  27.4 us
    all_gather x1, waiting for transfers between devices, body(): lax.all_gather(keys, 'seq', axis=1, tiled=True)  21.7 us
  transfers between devices with their start and end apart: 10, of which 9 were waited for; matrix products, arithmetic and copies ran while one was open for 8% of the time, Pallas kernels for 0%

commit v1 on v0

v1 whole, which is shorter than its diff:
```python
import jax
import jax.numpy as jnp
from jax import lax
from jax.experimental import pallas as pl
from jax.experimental.pallas import tpu as pltpu
from jax.sharding import PartitionSpec as P

HS = 64
EPS = 1e-06
BF = jnp.bfloat16
F32 = jnp.float32
LANES = 128
MIB = 1024 * 1024
VMEM = pl.BlockSpec(memory_space=pltpu.VMEM)
ANY = pl.BlockSpec(memory_space=pl.ANY)
SMEM = pl.BlockSpec(memory_space=pltpu.SMEM)


def dot(a, b, ca, cb):
    return lax.dot_general(a, b, (((ca,), (cb,)), ((), ())), preferred_element_type=F32)


def block(index, size):
    return pl.ds(pl.multiple_of(index * size, size), size)


def lane_block(p):
    return slice(p * LANES, (p + 1) * LANES)


def call(kernel, outs, scratch=(), smem=1, left=0, vmem=28 * MIB):
    def run(*args):
        return pl.pallas_call(
            kernel,
            out_shape=[jax.ShapeDtypeStruct(s, d) for s, d in outs],
            in_specs=[SMEM] * smem + [ANY] * left + [VMEM] * (len(args) - smem - left),
            out_specs=[VMEM] * len(outs),
            scratch_shapes=list(scratch),
            compiler_params=pltpu.CompilerParams(vmem_limit_bytes=vmem),
            cost_estimate=pl.CostEstimate(flops=1, bytes_accessed=1, transcendentals=0),
        )(*args)

    return run


def send(x, axis, offset):
    size = lax.axis_size(axis)
    return lax.ppermute(x, axis, [(i, i ^ offset) for i in range(size)])


def after(xs, deps):
    return lax.optimization_barrier((xs, deps))[0]


def segment_mean(x):
    low = lax.broadcasted_iota(jnp.int32, x.shape, 1) < HS
    first = jnp.sum(jnp.where(low, x, 0.0), axis=-1, keepdims=True)
    second = jnp.sum(jnp.where(low, 0.0, x), axis=-1, keepdims=True)
    return jnp.where(low, first, second) * (1.0 / HS)


def norm_fwd(x):
    centred = x - segment_mean(x)
    inverse = lax.rsqrt(segment_mean(centred * centred) + EPS)
    return centred * inverse, inverse


def norm_bwd(upstream, normed, inverse, gain):
    scaled = upstream * gain
    return inverse * (scaled - segment_mean(scaled) - normed * segment_mean(scaled * normed))


def prepare_kernel(keys, values, rows, cot, gain, both, out, khat, kinv, held, sems):
    width = keys.shape[1]
    copies = [
        pltpu.make_async_copy(keys, held, sems.at[0]),
        pltpu.make_async_copy(values, out.at[:, pl.ds(width, width)], sems.at[1]),
        pltpu.make_async_copy(rows, both.at[0], sems.at[2]),
        pltpu.make_async_copy(cot, both.at[1], sems.at[3]),
    ]
    for copy in copies:
        copy.start()
    copies[0].wait()
    for p in range(width // LANES):
        at = lane_block(p)
        hat, inv = norm_fwd(held[:, at].astype(F32))
        khat[:, at] = hat
        kinv[:, at] = inv
        out[:, at] = (hat * gain[:, at]).astype(BF)
    for copy in copies[1:]:
        copy.wait()


def query_kernel(place, w, *refs):
    x, out = refs[:8], refs[8]
    t = place[1]
    width = x[0].shape[2]
    total = None
    for j in range(8):
        part = dot(x[j][0], w[block(t ^ j, width), :], 1, 0)
        total = part if total is None else total + part
    out[...] = total


def gradient_kernel(place, w, *refs):
    x, out = refs[:8], refs[8]
    t = place[1]
    width = x[0].shape[2]
    total = None
    for j in range(8):
        part = dot(w[:, block(t ^ j, width)], x[j][1], 1, 1)
        total = part if total is None else total + part
    out[...] = jnp.transpose(total).astype(BF)


def cut_kernel(place, *refs):
    x, outs = refs[:4], refs[4:]
    s = place[0]
    for k, out in enumerate(outs):
        for i in range(4):
            for which in range(2):
                out[4 * which + i] = jnp.transpose(x[i][which, :, block(s ^ (k + 1), LANES)])


def forward_kernel(place, counts, source, target, qgain, query, *refs):
    kv, out, probs_out, keys, values, normed, qhat, qinv, ids = refs[:4], *refs[4:]
    s = place[0]
    rows, width = query.shape
    own = kv[0].shape[0]
    for k in range(4):
        keys[k * own : (k + 1) * own, :] = kv[k][:, :width]
        values[k * own : (k + 1) * own, :] = kv[k][:, width:]
        ids[:, k * own : (k + 1) * own] = source[:, block(s ^ k, own)]
    mine = jnp.transpose(jnp.broadcast_to(target[...].astype(F32), (rows, rows)))[:, :1]
    allowed = mine == ids[...].astype(F32)
    live = (lax.broadcasted_iota(jnp.int32, (rows, 1), 0) < counts[0, s]).astype(F32)
    low = lax.broadcasted_iota(jnp.int32, (rows, LANES), 1) < HS
    for p in range(width // LANES):
        at = lane_block(p)
        hat, inv = norm_fwd(query[:, at])
        qhat[:, at] = hat
        qinv[:, at] = inv
        q = (hat * qgain[:, at]).astype(BF)
        normed[:, at] = q
        zero = jnp.zeros_like(q)
        attended = []
        for h in range(2):
            head = low if h == 0 else jnp.logical_not(low)
            scores = dot(jnp.where(head, q, zero), keys[:, at], 1, 1)
            scores = jnp.where(allowed, scores, -jnp.inf)
            expo = jnp.exp(scores - jnp.max(scores, axis=-1, keepdims=True))
            probs = expo * (live / jnp.sum(expo, axis=-1, keepdims=True))
            probs_out[2 * p + h] = probs
            attended.append(dot(probs.astype(BF), values[:, at], 1, 0).astype(BF))
        out[:, at] = jnp.where(low, attended[0], attended[1])


def backward_kernel(qgain, grad, attended, probs, keys, values, qhat, qinv, out, sgrads):
    rows, width = grad.shape
    out[:, :width] = attended[...]
    low = lax.broadcasted_iota(jnp.int32, (rows, LANES), 1) < HS
    for p in range(width // LANES):
        at = lane_block(p)
        g = grad[:, at]
        zero = jnp.zeros_like(g)
        upstream = []
        for h in range(2):
            gh = jnp.where(low if h == 0 else jnp.logical_not(low), g, zero)
            delta = jnp.sum(gh.astype(F32) * attended[:, at].astype(F32), axis=-1, keepdims=True)
            sgrad = (probs[2 * p + h] * (dot(gh, values[:, at], 1, 1) - delta)).astype(BF)
            sgrads[2 * p + h] = sgrad
            upstream.append(dot(sgrad, keys[:, at], 1, 0))
        dq = jnp.where(low, upstream[0], upstream[1])
        out[:, lane_block(p + width // LANES)] = norm_bwd(dq, qhat[:, at], qinv[:, at], qgain[:, at]).astype(BF)


def partial_kernel(grad, normed, probs, sgrads, *outs):
    width = grad.shape[1]
    own = outs[0].shape[0]
    wide = lax.broadcasted_iota(jnp.int32, (4 * own, LANES), 1) < HS
    for p in range(width // LANES):
        at, other = lane_block(p), lane_block(p + width // LANES)
        dk = [dot(sgrads[2 * p + h], normed[:, at], 0, 0) for h in range(2)]
        dv = [dot(probs[2 * p + h].astype(BF), grad[:, at], 0, 0) for h in range(2)]
        dk = jnp.where(wide, dk[0], dk[1]).astype(BF)
        dv = jnp.where(wide, dv[0], dv[1]).astype(BF)
        for k, out in enumerate(outs):
            out[:, at] = dk[k * own : (k + 1) * own]
            out[:, other] = dv[k * own : (k + 1) * own]


def product_kernel(place, w_output, w_query, both, keep, other):
    t = place[1]
    width = w_query.shape[1]
    attended, query_grad = both[:, :width], both[:, width:]
    for j in range(8):
        out, i = (other if j % 2 else keep), j // 2
        out[0, i] = dot(attended, w_output[:, block(t ^ j, width)], 1, 0).astype(BF)
        part = dot(w_query[block(t ^ j, width), :], query_grad, 1, 1).astype(BF)
        out[1, i] = jnp.transpose(part)


def pair_kernel(keep, got, *outs):
    for i, out in enumerate(outs):
        out[...] = (keep[:, i].astype(F32) + got[:, i].astype(F32)).astype(BF)


def weight_kernel(place, *refs):
    x, parts, tiles, outs, full, across = refs[:8], refs[8:12], refs[12:18], refs[18:22], refs[22], refs[23]
    s, t, d = place[0], place[1], place[2]
    rows = parts[0].shape[0]
    width = x[0].shape[2]
    for k in range(4):
        full[k * rows : (k + 1) * rows, :] = parts[k][...]
    for which in range(2):
        for j in range(8):
            to = block((t ^ d) ^ j, LANES)
            across[which, to, :rows] = jnp.transpose(x[j][which, :, block(s, LANES)])
        for k in range(1, 4):
            at = slice(k * rows, (k + 1) * rows)
            for side in range(2):
                for i in range(4):
                    to = block((t ^ d) ^ (2 * i + side), LANES)
                    across[which, to, at] = tiles[2 * (k - 1) + side][4 * which + i]
    for m, out in enumerate(outs):
        for z in range(2):
            at = lane_block(2 * m + z)
            out[z, 0] = dot(across[0, at, :], full[:, width:], 1, 0).astype(BF)
            out[z, 1] = dot(across[1, at, :], full[:, :width], 1, 0).astype(BF)


def source_kernel(gain, khat, kinv, *refs):
    parts, keys, values = refs[:4], refs[4], refs[5]
    width = keys.shape[1]
    for p in range(width // LANES):
        at, other = lane_block(p), lane_block(p + width // LANES)
        dk = sum(part[:, at].astype(F32) for part in parts)
        dv = sum(part[:, other].astype(F32) for part in parts)
        keys[:, at] = norm_bwd(dk, khat[:, at], kinv[:, at], gain[:, at]).astype(BF)
        values[:, at] = dv.astype(BF)


def share(x):
    return [x] + [send(x, "seq", k) for k in range(1, 4)]


def total_of(parts):
    return sum(part.astype(F32) for part in parts)


def body(
    rows,
    keys,
    values,
    target_ids,
    source_ids,
    row_counts,
    w_query,
    w_output,
    query_gain,
    key_gain,
    cotangent,
):
    tokens, width = rows.shape[1:]
    own = keys.shape[1]
    place = jnp.stack([lax.axis_index("seq"), lax.axis_index("tensor"), lax.axis_index("dp")])
    place = place.astype(jnp.int32)
    qgain, kgain = query_gain.reshape(1, -1), key_gain.reshape(1, -1)
    line = (tokens, width)

    own_block, message, khat, kinv = call(
        prepare_kernel,
        [((2, tokens, width), BF), ((own, 2 * width), BF), ((own, width), F32), ((own, width), F32)],
        [pltpu.VMEM((own, width), BF), pltpu.SemaphoreType.DMA((4,))],
        smem=0,
        left=4,
        vmem=60 * MIB,
    )(keys[0], values[0], rows[0], cotangent[0], kgain)
    kv = share(message)
    even = [own_block] + [send(after(own_block, kv[3]) if i == 1 else own_block, "tensor", 2 * i) for i in range(1, 4)]
    even = [even[0], even[1], *after(even[2:], kv[1:3])]
    blocks = [b for e in even for b in (e, send(e, "tensor", 1))]
    query = call(query_kernel, [(line, F32)])(place, w_query, *blocks)[0]
    grad = call(gradient_kernel, [(line, BF)])(place, w_output, *blocks)[0]
    cut = call(cut_kernel, [((8, LANES, tokens), BF)] * 3)(place, *even)
    cut = [send(tile, "seq", k + 1) for k, tile in enumerate(cut)]
    tiles = [half for tile in cut for half in (tile, send(tile, "tensor", 1))]

    attended, probs, keys_all, values_all, normed, qhat, qinv = call(
        forward_kernel,
        [(line, BF), ((2 * width // LANES, tokens, 4 * own), F32), ((4 * own, width), BF), ((4 * own, width), BF)]
        + [(line, BF), (line, F32), (line, F32)],
        [pltpu.VMEM((1, 4 * own), jnp.int32)],
        smem=2,
    )(place, row_counts, source_ids, target_ids, qgain, query, *kv)
    both, sgrads = call(
        backward_kernel,
        [((tokens, 2 * width), BF), ((2 * width // LANES, tokens, 4 * own), BF)],
        smem=0,
    )(qgain, grad, attended, probs, keys_all, values_all, qhat, qinv)
    parts = share(both)
    kv_parts = call(partial_kernel, [((own, 2 * width), BF)] * 4, smem=0)(
        grad, normed, probs, after(sgrads, cut)
    )

    keep, other = call(product_kernel, [((2, 4, tokens, width), BF)] * 2)(
        place, w_output, w_query, after(both, cut)
    )
    got = send(after(other, parts[1]), "tensor", 1)
    pairs = call(pair_kernel, [((2, tokens, width), BF)] * 4, smem=0)(keep, got)
    lines = [pairs[0]] + [send(pairs[i], "tensor", 2 * i) for i in range(1, 4)]
    sums = call(
        weight_kernel,
        [((2, 2, LANES, width), BF)] * 4,
        [pltpu.VMEM((4 * tokens, 2 * width), BF), pltpu.VMEM((2, 8 * LANES, 4 * tokens), BF)],
    )(place, *blocks, *after(parts, (kv_parts, lines[1], lines[2])), *tiles)
    sums = total_of([sums[0]] + [send(sums[m], "dp", 2 * m) for m in range(1, 4)])
    lines = total_of(lines).astype(BF)
    kv_sums = [kv_parts[0]] + [send(after(kv_parts[k], lines), "seq", k) for k in (1, 3, 2)]
    weights = sums[0] + send(sums[1].astype(BF), "dp", 1).astype(F32)
    keys_grad, values_grad = call(source_kernel, [((own, width), BF)] * 2, smem=0)(
        kgain, khat, kinv, *kv_sums
    )
    return (
        lines[:1],
        lines[1:],
        keys_grad[None],
        values_grad[None],
        weights[0],
        weights[1].T,
    )


def solution(mesh):
    in_specs = (
        P("dp", "seq", "tensor"),
        P("dp", "seq", "tensor"),
        P("dp", "seq", "tensor"),
        P("dp", "seq"),
        P("dp", None),
        P("dp", None),
        P(None, "tensor"),
        P("tensor", None),
        P("tensor"),
        P("tensor"),
        P("dp", "seq", "tensor"),
    )
    out_specs = (
        P("dp", "seq", "tensor"),
        P("dp", "seq", "tensor"),
        P("dp", "seq", "tensor"),
        P("dp", "seq", "tensor"),
        P(("dp", "seq"), "tensor"),
        P("tensor", ("dp", "seq")),
    )
    return jax.shard_map(body, mesh=mesh, in_specs=in_specs, out_specs=out_specs, check_vma=False)
```

time: 833 us -> 130 us (0.16)
  waiting for transfers between devices: 669 us -> 62.8 us
  matrix products: 84.5 us -> 0 us
  starting transfers between devices: 0.4 us -> 37.3 us
  local copies, waits for them, and re-layouts: 31.9 us -> 5.67 us
  other arithmetic: 24.7 us -> 0.53 us
  Pallas kernels: 0 us -> 22.5 us
  between operations: 14.4 us -> 0.93 us
    unnamed x12 -> x0, waiting for transfers between devices: 469 us -> none
    all_gather x4 -> x0, waiting for transfers between devices: 114 us -> none  [the longest x1 33.1 us: body(): lax.all_gather(rows, 'tensor', axis=2, tiled=True)]
    reduce_scatter x4 -> x0, waiting for transfers between devices: 85.9 us -> none  [the longest x1 39.6 us: body(): lax.psum_scatter(x_part[None].astype(jnp.bfloat16), 'tensor', scatter_dim...]
    dot_general x54 -> x0, matrix products: 84.5 us -> none  [the longest x8 13.4 us: head_work(): lax.dot_general(plow, g_head, inner, preferred_element_type=jnp.float32)]
    ppermute x0 -> x30, waiting for transfers between devices: none -> 62.8 us  [send(): return lax.ppermute(x, axis, [(i, i ^ offset) for i in range(size)])]
    ppermute x0 -> x30, starting transfers between devices: none -> 37.3 us  [send(): return lax.ppermute(x, axis, [(i, i ^ offset) for i in range(size)])]
    unnamed x22 -> x27, local copies, waits for them, and re-layouts: 30.3 us -> 4.18 us
    pallas_call x0 -> x11, Pallas kernels: none -> 22.5 us  [run(): pl.pallas_call(kernel, out_shape=[jax.ShapeDtypeStruct(s, d) for s, d in...]
  transfers between devices with their start and end apart: 10 -> 30, of which waited for: 9 -> 12; matrix products, arithmetic and copies ran while one was open for 8% -> 1% of each run, Pallas kernels for 0% -> 13%
where the time goes in v1:
time: 130 us
  waiting for transfers between devices  62.8 us (48%)
  starting transfers between devices  37.3 us (29%)
  Pallas kernels  22.5 us (17%)
  local copies, waits for them, and re-layouts  5.67 us (4%)
    ppermute x30, waiting for transfers between devices, send(): return lax.ppermute(x, axis, [(i, i ^ offset) for i in range(size)])  62.8 us
    ppermute x30, starting transfers between devices, send(): return lax.ppermute(x, axis, [(i, i ^ offset) for i in range(size)])  37.3 us
    pallas_call x11, Pallas kernels, run(): pl.pallas_call(kernel, out_shape=[jax.ShapeDtypeStruct(s, d) for s, d in...  22.5 us
    unnamed x27, local copies, waits for them, and re-layouts  4.18 us
  transfers between devices with their start and end apart: 30, of which 12 were waited for; matrix products, arithmetic and copies ran while one was open for 1% of the time, Pallas kernels for 13%

profile of v1, /device:TPU:32, one launch (start us, length us, event | category | flops | bytes accessed | tf_op | source)
XLA Modules:
  0.0 129.7 jit_solution(16893388021379914825)
XLA Ops:
  0.6 3.8 %shard_map.154 = (bf16[2,128,512]{2,1,0:T(8,128)(2,1)}, bf16[256,1024]{1,0:T(8,128)(2,1)}, f32[256,512]{1,0:T(8,128)}, f32[256,512]{1,0:T(8,128)}) custom-call(bf16[256,512]{1,0:T(8,128)(2,1)} %bitcast.27, bf16[256,512]{1,0:T(8,128)(2,1)} %bitcast.28, bf16[128,512]{1,0:T(8,128)(2,1)} %bitcast.29, bf16[128,512]{1,0:T(8,128)(2,1)} %bitcast.30, f32[1,512]{1,0:T(1,128)} %bitcast.23), custom_call_target="tpu_custom_call" | custom-call | flops 1 | bytes 1 | tf_op jit(solution)/shard_map/pallas_call | solution.py:33
  4.4 2.8 %collective-permute-start.1 = (bf16[256,1024]{1,0:T(8,128)(2,1)}, bf16[256,1024]{1,0:T(8,128)(2,1)S(1)}, u32[]{:S(2)}, u32[]{:S(2)}) collective-permute-start(bf16[256,1024]{1,0:T(8,128)(2,1)} %get-tuple-element.52.refs_0_), channel_id=1, source_target_pairs={{0,24},{8,16},{16,8},{24,0},{1,25},{9,17},{17,9},{25,1},{2,26},{10... | collective-permute-start | bytes 1572872 | tf_op jit(solution)/shard_map/ppermute | solution.py:48
  7.5 1.7 %collective-permute-start.7 = (bf16[256,1024]{1,0:T(8,128)(2,1)}, bf16[256,1024]{1,0:T(8,128)(2,1)S(1)}, u32[]{:S(2)}, u32[]{:S(2)}) collective-permute-start(bf16[256,1024]{1,0:T(8,128)(2,1)} %get-tuple-element.52.refs_0_), channel_id=1, source_target_pairs={{0,16},{8,24},{16,0},{24,8},{1,17},{9,25},{17,1},{25,9},{2,18},{10... | collective-permute-start | bytes 1572872 | tf_op jit(solution)/shard_map/ppermute | solution.py:48
  9.2 3.3 %collective-permute-start.4 = (bf16[2,128,512]{2,1,0:T(8,128)(2,1)}, bf16[2,128,512]{2,1,0:T(8,128)(2,1)S(1)}, u32[]{:S(2)}, u32[]{:S(2)}) collective-permute-start(bf16[2,128,512]{2,1,0:T(8,128)(2,1)} %get-tuple-element.53.refs_0_), channel_id=1, source_target_pairs={{0,4},{1,5},{2,6},{3,7},{4,0},{5,1},{6,2},{7,3},{8,12},{9,13},{10,... | collective-permute-start | bytes 786440 | tf_op jit(solution)/shard_map/ppermute | solution.py:48
  12.5 7.4 %collective-permute-done.1.refs_3_ = bf16[256,1024]{1,0:T(8,128)(2,1)S(1)} collective-permute-done((bf16[256,1024]{1,0:T(8,128)(2,1)}, bf16[256,1024]{1,0:T(8,128)(2,1)S(1)}, u32[]{:S(2)}, u32[]{:S(2)}) %collective-permute-start.1) | collective-permute-done | bytes 524320 | tf_op jit(solution)/shard_map/ppermute | solution.py:48
  19.8 1.7 %collective-permute-start.2 = (bf16[2,128,512]{2,1,0:T(8,128)(2,1)}, bf16[2,128,512]{2,1,0:T(8,128)(2,1)S(1)}, u32[]{:S(2)}, u32[]{:S(2)}) collective-permute-start(bf16[2,128,512]{2,1,0:T(8,128)(2,1)} %get-tuple-element.53.refs_0_), channel_id=1, source_target_pairs={{0,2},{1,3},{2,0},{3,1},{4,6},{5,7},{6,4},{7,5},{8,10},{9,11},{10,... | collective-permute-start | bytes 786440 | tf_op jit(solution)/shard_map/ppermute | solution.py:48
  21.5 6.9 %collective-permute-done.4.refs_4_.refs_2_ = bf16[2,128,512]{2,1,0:T(8,128)(2,1)S(1)} collective-permute-done((bf16[2,128,512]{2,1,0:T(8,128)(2,1)}, bf16[2,128,512]{2,1,0:T(8,128)(2,1)S(1)}, u32[]{:S(2)}, u32[]{:S(2)}) %collective-permute-start.4) | collective-permute-done | bytes 262176 | tf_op jit(solution)/shard_map/ppermute | solution.py:48
  28.4 5.5 %collective-permute-done.5.refs_6_.refs_3_ = bf16[2,128,512]{2,1,0:T(8,128)(2,1)S(1)} collective-permute-done((bf16[2,128,512]{2,1,0:T(8,128)(2,1)}, bf16[2,128,512]{2,1,0:T(8,128)(2,1)S(1)}, u32[]{:S(2)}, u32[]{:S(2)}) %collective-permute-start.5) | collective-permute-done | bytes 262176 | tf_op jit(solution)/shard_map/ppermute | solution.py:48
  37.0 3.9 %collective-permute-start.11 = (bf16[8,128,128]{2,1,0:T(8,128)(2,1)S(1)}, bf16[8,128,128]{2,1,0:T(8,128)(2,1)S(1)}, u32[]{:S(2)}, u32[]{:S(2)}) collective-permute-start(bf16[8,128,128]{2,1,0:T(8,128)(2,1)S(1)} %get-tuple-element.64), channel_id=1, source_target_pairs={{0,16},{8,24},{16,0},{24,8},{1,17},{9,25},{17,1},{25,9},{2,18},{10... | collective-permute-start | bytes 786440 | tf_op jit(solution)/shard_map/ppermute | solution.py:48
  41.3 2.2 %copy-done.1 = bf16[4096,512]{1,0:T(8,128)(2,1)S(1)} copy-done((bf16[4096,512]{1,0:T(8,128)(2,1)S(1)}, bf16[4096,512]{1,0:T(8,128)(2,1)}, u32[]{:S(2)}) %copy-start.1) | copy-done | bytes 4194328
  44.9 1.9 %shard_map.155.grad = bf16[128,512]{1,0:T(8,128)(2,1)S(1)} custom-call(s32[3]{0:T(128)S(1)} %pad_add_fusion.place, bf16[512,4096]{1,0:T(8,128)(2,1)S(1)} %copy-done, bf16[2,128,512]{2,1,0:T(8,128)(2,1)S(1)} %copy-done.3, bf16[2,128,512]{2,1,0:T(8,128)(2,1)S(1)} %collective-permute-done.refs_1_, ...), custom_call_target="tpu_custom_call" | custom-call | flops 1 | bytes 1 | tf_op jit(solution)/shard_map/pallas_call | solution.py:33
  46.8 4.8 %shard_map.157 = (bf16[128,512]{1,0:T(8,128)(2,1)S(1)}, f32[8,128,1024]{2,1,0:T(8,128)S(1)}, bf16[1024,512]{1,0:T(8,128)(2,1)S(1)}, bf16[1024,512]{1,0:T(8,128)(...) custom-call(s32[3]{0:T(128)S(1)} %pad_add_fusion.place, ...), custom_call_target="tpu_custom_call" | custom-call | flops 1 | bytes 1 | tf_op jit(solution)/shard_map/pallas_call | solution.py:33
  51.6 2.0 %shard_map.158 = (bf16[128,1024]{1,0:T(8,128)(2,1)S(1)}, bf16[8,128,1024]{2,1,0:T(8,128)(2,1)S(1)}) custom-call(f32[1,512]{1,0:T(1,128)S(1)} %bitcast.26, bf16[128,512]{1,0:T(8,128)(2,1)S(1)} %shard_map.155.grad, bf16[128,512]{1,0:T(8,128)(2,1)S(1)} %get-tuple-element.56.attended, f32[8,128,1024]{2,1,0:T(8,128)S(1)} %get-tuple-element.57.probs, ...), custom_call_target="tpu_custom_call" | custom-call | flops 1 | bytes 1 | tf_op jit(solution)/shard_map/pallas_call | solution.py:33
  53.7 2.0 %collective-permute-done.12.refs_16_ = bf16[8,128,128]{2,1,0:T(8,128)(2,1)S(1)} collective-permute-done((bf16[8,128,128]{2,1,0:T(8,128)(2,1)S(1)}, bf16[8,128,128]{2,1,0:T(8,128)(2,1)S(1)}, u32[]{:S(2)}, u32[]{:S(2)}) %collective-permute-start.12) | collective-permute-done | bytes 262176 | tf_op jit(solution)/shard_map/ppermute | solution.py:48
  55.8 2.5 %shard_map.160 = (bf16[2,4,128,512]{3,2,1,0:T(8,128)(2,1)S(1)}, bf16[2,4,128,512]{3,2,1,0:T(8,128)(2,1)S(1)}) custom-call(s32[3]{0:T(128)S(1)} %pad_add_fusion.place, bf16[512,4096]{1,0:T(8,128)(2,1)S(1)} %copy-done, bf16[4096,512]{1,0:T(8,128)(2,1)S(1)} %copy-done.2, bf16[128,1024]{1,0:T(8,128)(2,1)S(1)} %get-tuple-element.88.both.refs_8_), custom_call_target="tpu_custom_call" | custom-call | flops 1 | bytes 1 | tf_op jit(solution)/shard_map/pallas_call | solution.py:33
  58.2 3.3 %collective-permute-done.13.refs_9_ = bf16[128,1024]{1,0:T(8,128)(2,1)S(1)} collective-permute-done((bf16[128,1024]{1,0:T(8,128)(2,1)S(1)}, bf16[128,1024]{1,0:T(8,128)(2,1)S(1)}, u32[]{:S(2)}, u32[]{:S(2)}) %collective-permute-start.13) | collective-permute-done | bytes 262176 | tf_op jit(solution)/shard_map/ppermute | solution.py:48
  61.5 2.5 %collective-permute-start.21 = (bf16[128,1024]{1,0:T(8,128)(2,1)S(1)}, bf16[128,1024]{1,0:T(8,128)(2,1)S(1)}, u32[]{:S(2)}, u32[]{:S(2)}) collective-permute-start(bf16[128,1024]{1,0:T(8,128)(2,1)S(1)} %get-tuple-element.88.both.refs_8_), channel_id=1, source_target_pairs={{0,16},{8,24},{16,0},{24,8},{1,17},{9,25},{17,1},{25,9},{2,18},{10... | collective-permute-start | bytes 786440 | tf_op jit(solution)/shard_map/ppermute | solution.py:48
  65.4 3.2 %collective-permute-start.16 = (bf16[2,128,512]{2,1,0:T(8,128)(2,1)S(1)}, bf16[2,128,512]{2,1,0:T(8,128)(2,1)S(1)}, u32[]{:S(2)}, u32[]{:S(2)}) collective-permute-start(bf16[2,128,512]{2,1,0:T(8,128)(2,1)S(1)} %get-tuple-element.72), channel_id=1, source_target_pairs={{0,4},{1,5},{2,6},{3,7},{4,0},{5,1},{6,2},{7,3},{8,12},{9,13},{10,... | collective-permute-start | bytes 786440 | tf_op jit(solution)/shard_map/ppermute | solution.py:48
  68.7 3.2 %collective-permute-done.21.refs_10_ = bf16[128,1024]{1,0:T(8,128)(2,1)S(1)} collective-permute-done((bf16[128,1024]{1,0:T(8,128)(2,1)S(1)}, bf16[128,1024]{1,0:T(8,128)(2,1)S(1)}, u32[]{:S(2)}, u32[]{:S(2)}) %collective-permute-start.21) | collective-permute-done | bytes 262176 | tf_op jit(solution)/shard_map/ppermute | solution.py:48
  71.8 5.5 %collective-permute-done.22.refs_11_ = bf16[128,1024]{1,0:T(8,128)(2,1)S(1)} collective-permute-done((bf16[128,1024]{1,0:T(8,128)(2,1)S(1)}, bf16[128,1024]{1,0:T(8,128)(2,1)S(1)}, u32[]{:S(2)}, u32[]{:S(2)}) %collective-permute-start.22) | collective-permute-done | bytes 262176 | tf_op jit(solution)/shard_map/ppermute | solution.py:48
  77.4 1.3 shard_map.162
  78.7 1.8 %collective-permute-done.16 = bf16[2,128,512]{2,1,0:T(8,128)(2,1)S(1)} collective-permute-done((bf16[2,128,512]{2,1,0:T(8,128)(2,1)S(1)}, bf16[2,128,512]{2,1,0:T(8,128)(2,1)S(1)}, u32[]{:S(2)}, u32[]{:S(2)}) %collective-permute-start.16) | collective-permute-done | bytes 262176 | tf_op jit(solution)/shard_map/ppermute | solution.py:48
  80.5 2.3 %shard_map.164 = (bf16[2,2,128,512]{3,2,1,0:T(8,128)(2,1)S(1)}, bf16[2,2,128,512]{3,2,1,0:T(8,128)(2,1)S(1)}, bf16[2,2,128,512]{3,2,1,0:T(8,128)(2,1)S(1)}, bf16[2,2,128,512]{3,2,1,0:T(8,128)(2,1)S(1)}) custom-call(s32[3]{0:T(128)S(1)} %pad_add_fusion.place, bf16[2,128,512]{2,1,0:T(8,128)(2,1)S(1)} %copy-done.4, ...), custom_call_target="tpu_custom_call" | custom-call | flops 1 | bytes 1 | tf_op jit(solution)/shard_map/pallas_call | solution.py:33
  82.8 1.7 %collective-permute-start.26 = (bf16[2,2,128,512]{3,2,1,0:T(8,128)(2,1)S(1)}, bf16[2,2,128,512]{3,2,1,0:T(8,128)(2,1)S(1)}, u32[]{:S(2)}, u32[]{:S(2)}) collective-permute-start(bf16[2,2,128,512]{3,2,1,0:T(8,128)(2,1)S(1)} %get-tuple-element.93), channel_id=1, source_target_pairs={{0,64},{32,96},{64,0},{96,32},{128,192},{160,224},{192,128},{224,1... | collective-permute-start | bytes 1572872 | tf_op jit(solution)/shard_map/ppermute | solution.py:48
  84.5 2.9 %collective-permute-start.27 = (bf16[2,2,128,512]{3,2,1,0:T(8,128)(2,1)S(1)}, bf16[2,2,128,512]{3,2,1,0:T(8,128)(2,1)S(1)}, u32[]{:S(2)}, u32[]{:S(2)}) collective-permute-start(bf16[2,2,128,512]{3,2,1,0:T(8,128)(2,1)S(1)} %get-tuple-element.94), channel_id=1, source_target_pairs={{0,128},{32,160},{64,192},{96,224},{128,0},{160,32},{192,64},{224,... | collective-permute-start | bytes 1572872 | tf_op jit(solution)/shard_map/ppermute | solution.py:48
  88.3 11.7 %collective-permute-done.17 = bf16[2,128,512]{2,1,0:T(8,128)(2,1)S(1)} collective-permute-done((bf16[2,128,512]{2,1,0:T(8,128)(2,1)S(1)}, bf16[2,128,512]{2,1,0:T(8,128)(2,1)S(1)}, u32[]{:S(2)}, u32[]{:S(2)}) %collective-permute-start.17) | collective-permute-done | bytes 262176 | tf_op jit(solution)/shard_map/ppermute | solution.py:48
  100.2 2.4 %collective-permute-start.20 = (bf16[256,1024]{1,0:T(8,128)(2,1)S(1)}, bf16[256,1024]{1,0:T(8,128)(2,1)S(1)}, u32[]{:S(2)}, u32[]{:S(2)}) collective-permute-start(bf16[256,1024]{1,0:T(8,128)(2,1)S(1)} %get-tuple-element.85), channel_id=1, source_target_pairs={{0,16},{8,24},{16,0},{24,8},{1,17},{9,25},{17,1},{25,9},{2,18},{10... | collective-permute-start | bytes 1572872 | tf_op jit(solution)/shard_map/ppermute | solution.py:48
  103.8 5.9 %collective-permute-done.27 = bf16[2,2,128,512]{3,2,1,0:T(8,128)(2,1)S(1)} collective-permute-done((bf16[2,2,128,512]{3,2,1,0:T(8,128)(2,1)S(1)}, bf16[2,2,128,512]{3,2,1,0:T(8,128)(2,1)S(1)}, u32[]{:S(2)}, u32[]{:S(2)}) %collective-permute-start.27) | collective-permute-done | bytes 524320 | tf_op jit(solution)/shard_map/ppermute | solution.py:48
  109.7 2.6 %collective-permute-done.28 = bf16[2,2,128,512]{3,2,1,0:T(8,128)(2,1)S(1)} collective-permute-done((bf16[2,2,128,512]{3,2,1,0:T(8,128)(2,1)S(1)}, bf16[2,2,128,512]{3,2,1,0:T(8,128)(2,1)S(1)}, u32[]{:S(2)}, u32[]{:S(2)}) %collective-permute-start.28) | collective-permute-done | bytes 524320 | tf_op jit(solution)/shard_map/ppermute | solution.py:48
  112.6 5.9 %collective-permute-start.29 = (bf16[2,128,512]{2,1,0:T(8,128)(2,1)S(1)}, bf16[2,128,512]{2,1,0:T(8,128)(2,1)S(1)}, u32[]{:S(2)}, u32[]{:S(2)}) collective-permute-start(bf16[2,128,512]{2,1,0:T(8,128)(2,1)S(1)} %fusion.1), channel_id=1, source_target_pairs={{0,32},{32,0},{64,96},{96,64},{128,160},{160,128},{192,224},{224,1... | collective-permute-start | bytes 786440 | tf_op jit(solution)/shard_map/ppermute | solution.py:48
  119.2 7.0 %collective-permute-done.19.refs_2_ = bf16[256,1024]{1,0:T(8,128)(2,1)S(1)} collective-permute-done((bf16[256,1024]{1,0:T(8,128)(2,1)S(1)}, bf16[256,1024]{1,0:T(8,128)(2,1)S(1)}, u32[]{:S(2)}, u32[]{:S(2)}) %collective-permute-start.19) | collective-permute-done | bytes 524320 | tf_op jit(solution)/shard_map/ppermute | solution.py:48
  126.3 1.7 %shard_map.163 = (bf16[256,512]{1,0:T(8,128)(2,1)}, bf16[256,512]{1,0:T(8,128)(2,1)}) custom-call(f32[1,512]{1,0:T(1,128)S(1)} %bitcast.24, f32[256,512]{1,0:T(8,128)S(1)} %copy-done.5, f32[256,512]{1,0:T(8,128)S(1)} %copy-done.6, bf16[256,1024]{1,0:T(8,128)(2,1)S(1)} %get-tuple-element.79.refs_0_, bf16[256,1024]{1,0:T(8,128)(2,1)S(1)} %collective-permute-done.18.refs_1_, ...), custom_call_target="tpu_custom_call" | custom-call | flops 1 | bytes 1 | tf_op jit(solution)/shard_map/pallas_call | solution.py:33
  (73 shorter events, 11.7 us)
Async XLA Ops:
  4.4 15.5 %collective-permute-start.1 = (bf16[256,1024]{1,0:T(8,128)(2,1)}, bf16[256,1024]{1,0:T(8,128)(2,1)S(1)}, u32[]{:S(2)}, u32[]{:S(2)}) collective-permute-start(bf16[256,1024]{1,0:T(8,128)(2,1)} %get-tuple-element.52.refs_0_), channel_id=1, source_target_pairs={{0,24},{8,16},{16,8},{24,0},{1,25},{9,17},{17,9},{25,1},{2,26},{10... | collective-permute-start | bytes 1572872 | tf_op jit(solution)/shard_map/ppermute | solution.py:48
  7.2 26.7 %collective-permute-start.6 = (bf16[256,1024]{1,0:T(8,128)(2,1)}, bf16[256,1024]{1,0:T(8,128)(2,1)S(1)}, u32[]{:S(2)}, u32[]{:S(2)}) collective-permute-start(bf16[256,1024]{1,0:T(8,128)(2,1)} %get-tuple-element.52.refs_0_), channel_id=1, source_target_pairs={{0,8},{8,0},{16,24},{24,16},{1,9},{9,1},{17,25},{25,17},{2,10},{10... | collective-permute-start | bytes 1572872 | tf_op jit(solution)/shard_map/ppermute | solution.py:48
  7.5 26.5 %collective-permute-start.7 = (bf16[256,1024]{1,0:T(8,128)(2,1)}, bf16[256,1024]{1,0:T(8,128)(2,1)S(1)}, u32[]{:S(2)}, u32[]{:S(2)}) collective-permute-start(bf16[256,1024]{1,0:T(8,128)(2,1)} %get-tuple-element.52.refs_0_), channel_id=1, source_target_pairs={{0,16},{8,24},{16,0},{24,8},{1,17},{9,25},{17,1},{25,9},{2,18},{10... | collective-permute-start | bytes 1572872 | tf_op jit(solution)/shard_map/ppermute | solution.py:48
  9.2 19.2 %collective-permute-start.4 = (bf16[2,128,512]{2,1,0:T(8,128)(2,1)}, bf16[2,128,512]{2,1,0:T(8,128)(2,1)S(1)}, u32[]{:S(2)}, u32[]{:S(2)}) collective-permute-start(bf16[2,128,512]{2,1,0:T(8,128)(2,1)} %get-tuple-element.53.refs_0_), channel_id=1, source_target_pairs={{0,4},{1,5},{2,6},{3,7},{4,0},{5,1},{6,2},{7,3},{8,12},{9,13},{10,... | collective-permute-start | bytes 786440 | tf_op jit(solution)/shard_map/ppermute | solution.py:48
  12.5 21.5 %collective-permute-start.5 = (bf16[2,128,512]{2,1,0:T(8,128)(2,1)}, bf16[2,128,512]{2,1,0:T(8,128)(2,1)S(1)}, u32[]{:S(2)}, u32[]{:S(2)}) collective-permute-start(bf16[2,128,512]{2,1,0:T(8,128)(2,1)} %get-tuple-element.53.refs_0_), channel_id=1, source_target_pairs={{0,6},{1,7},{2,4},{3,5},{4,2},{5,3},{6,0},{7,1},{8,14},{9,15},{10,... | collective-permute-start | bytes 786440 | tf_op jit(solution)/shard_map/ppermute | solution.py:48
  19.8 14.6 %collective-permute-start.2 = (bf16[2,128,512]{2,1,0:T(8,128)(2,1)}, bf16[2,128,512]{2,1,0:T(8,128)(2,1)S(1)}, u32[]{:S(2)}, u32[]{:S(2)}) collective-permute-start(bf16[2,128,512]{2,1,0:T(8,128)(2,1)} %get-tuple-element.53.refs_0_), channel_id=1, source_target_pairs={{0,2},{1,3},{2,0},{3,1},{4,6},{5,7},{6,4},{7,5},{8,10},{9,11},{10,... | collective-permute-start | bytes 786440 | tf_op jit(solution)/shard_map/ppermute | solution.py:48
  28.4 8.6 %collective-permute-start = (bf16[2,128,512]{2,1,0:T(8,128)(2,1)}, bf16[2,128,512]{2,1,0:T(8,128)(2,1)S(1)}, u32[]{:S(2)}, u32[]{:S(2)}) collective-permute-start(bf16[2,128,512]{2,1,0:T(8,128)(2,1)} %get-tuple-element.53.refs_0_), channel_id=1, source_target_pairs={{0,1},{1,0},{2,3},{3,2},{4,5},{5,4},{6,7},{7,6},{8,9},{9,8},{10,11... | collective-permute-start | bytes 786440 | tf_op jit(solution)/shard_map/ppermute | solution.py:48
  33.9 6.9 %collective-permute-start.8 = (bf16[2,128,512]{2,1,0:T(8,128)(2,1)S(1)}, bf16[2,128,512]{2,1,0:T(8,128)(2,1)S(1)}, u32[]{:S(2)}, u32[]{:S(2)}) collective-permute-start(bf16[2,128,512]{2,1,0:T(8,128)(2,1)S(1)} %collective-permute-done.4.refs_4_.refs_2_), channel_id=1, source_target_pairs={{0,1},{1,0},{2,3},{3,2},{4,5},{5,4},{6,7},{7,6},{8,9},{9,8},{10,11... | collective-permute-start | bytes 786440 | tf_op jit(solution)/shard_map/ppermute | solution.py:48
  34.0 7.4 %collective-permute-start.9 = (bf16[2,128,512]{2,1,0:T(8,128)(2,1)S(1)}, bf16[2,128,512]{2,1,0:T(8,128)(2,1)S(1)}, u32[]{:S(2)}, u32[]{:S(2)}) collective-permute-start(bf16[2,128,512]{2,1,0:T(8,128)(2,1)S(1)} %collective-permute-done.5.refs_6_.refs_3_), channel_id=1, source_target_pairs={{0,1},{1,0},{2,3},{3,2},{4,5},{5,4},{6,7},{7,6},{8,9},{9,8},{10,11... | collective-permute-start | bytes 786440 | tf_op jit(solution)/shard_map/ppermute | solution.py:48
  34.5 6.9 %collective-permute-start.3 = (bf16[2,128,512]{2,1,0:T(8,128)(2,1)S(1)}, bf16[2,128,512]{2,1,0:T(8,128)(2,1)S(1)}, u32[]{:S(2)}, u32[]{:S(2)}) collective-permute-start(bf16[2,128,512]{2,1,0:T(8,128)(2,1)S(1)} %collective-permute-done.2.refs_2_.refs_1_), channel_id=1, source_target_pairs={{0,1},{1,0},{2,3},{3,2},{4,5},{5,4},{6,7},{7,6},{8,9},{9,8},{10,11... | collective-permute-start | bytes 786440 | tf_op jit(solution)/shard_map/ppermute | solution.py:48
  36.5 17.2 %collective-permute-start.10 = (bf16[8,128,128]{2,1,0:T(8,128)(2,1)S(1)}, bf16[8,128,128]{2,1,0:T(8,128)(2,1)S(1)}, u32[]{:S(2)}, u32[]{:S(2)}) collective-permute-start(bf16[8,128,128]{2,1,0:T(8,128)(2,1)S(1)} %get-tuple-element.63), channel_id=1, source_target_pairs={{0,8},{8,0},{16,24},{24,16},{1,9},{9,1},{17,25},{25,17},{2,10},{10... | collective-permute-start | bytes 786440 | tf_op jit(solution)/shard_map/ppermute | solution.py:48
  37.0 16.7 %collective-permute-start.11 = (bf16[8,128,128]{2,1,0:T(8,128)(2,1)S(1)}, bf16[8,128,128]{2,1,0:T(8,128)(2,1)S(1)}, u32[]{:S(2)}, u32[]{:S(2)}) collective-permute-start(bf16[8,128,128]{2,1,0:T(8,128)(2,1)S(1)} %get-tuple-element.64), channel_id=1, source_target_pairs={{0,16},{8,24},{16,0},{24,8},{1,17},{9,25},{17,1},{25,9},{2,18},{10... | collective-permute-start | bytes 786440 | tf_op jit(solution)/shard_map/ppermute | solution.py:48
  40.9 14.9 %collective-permute-start.12 = (bf16[8,128,128]{2,1,0:T(8,128)(2,1)S(1)}, bf16[8,128,128]{2,1,0:T(8,128)(2,1)S(1)}, u32[]{:S(2)}, u32[]{:S(2)}) collective-permute-start(bf16[8,128,128]{2,1,0:T(8,128)(2,1)S(1)} %get-tuple-element.65), channel_id=1, source_target_pairs={{0,24},{8,16},{16,8},{24,0},{1,25},{9,17},{17,9},{25,1},{2,26},{10... | collective-permute-start | bytes 786440 | tf_op jit(solution)/shard_map/ppermute | solution.py:48
  53.6 7.9 %collective-permute-start.13 = (bf16[128,1024]{1,0:T(8,128)(2,1)S(1)}, bf16[128,1024]{1,0:T(8,128)(2,1)S(1)}, u32[]{:S(2)}, u32[]{:S(2)}) collective-permute-start(bf16[128,1024]{1,0:T(8,128)(2,1)S(1)} %get-tuple-element.88.both.refs_8_), channel_id=1, source_target_pairs={{0,8},{8,0},{16,24},{24,16},{1,9},{9,1},{17,25},{25,17},{2,10},{10... | collective-permute-start | bytes 786440 | tf_op jit(solution)/shard_map/ppermute | solution.py:48
  61.5 3.0 %collective-permute-start.14 = (bf16[2,4,128,512]{3,2,1,0:T(8,128)(2,1)S(1)}, bf16[2,4,128,512]{3,2,1,0:T(8,128)(2,1)S(1)}, u32[]{:S(2)}, u32[]{:S(2)}) collective-permute-start(bf16[2,4,128,512]{3,2,1,0:T(8,128)(2,1)S(1)} %get-tuple-element.69), channel_id=1, source_target_pairs={{0,1},{1,0},{2,3},{3,2},{4,5},{5,4},{6,7},{7,6},{8,9},{9,8},{10,11... | collective-permute-start | bytes 3145736 | tf_op jit(solution)/shard_map/ppermute | solution.py:48
  61.5 10.3 %collective-permute-start.21 = (bf16[128,1024]{1,0:T(8,128)(2,1)S(1)}, bf16[128,1024]{1,0:T(8,128)(2,1)S(1)}, u32[]{:S(2)}, u32[]{:S(2)}) collective-permute-start(bf16[128,1024]{1,0:T(8,128)(2,1)S(1)} %get-tuple-element.88.both.refs_8_), channel_id=1, source_target_pairs={{0,16},{8,24},{16,0},{24,8},{1,17},{9,25},{17,1},{25,9},{2,18},{10... | collective-permute-start | bytes 786440 | tf_op jit(solution)/shard_map/ppermute | solution.py:48
  64.0 13.4 %collective-permute-start.22 = (bf16[128,1024]{1,0:T(8,128)(2,1)S(1)}, bf16[128,1024]{1,0:T(8,128)(2,1)S(1)}, u32[]{:S(2)}, u32[]{:S(2)}) collective-permute-start(bf16[128,1024]{1,0:T(8,128)(2,1)S(1)} %get-tuple-element.88.both.refs_8_), channel_id=1, source_target_pairs={{0,24},{8,16},{16,8},{24,0},{1,25},{9,17},{17,9},{25,1},{2,26},{10... | collective-permute-start | bytes 786440 | tf_op jit(solution)/shard_map/ppermute | solution.py:48
  64.7 14.0 %collective-permute-start.15 = (bf16[2,128,512]{2,1,0:T(8,128)(2,1)S(1)}, bf16[2,128,512]{2,1,0:T(8,128)(2,1)S(1)}, u32[]{:S(2)}, u32[]{:S(2)}) collective-permute-start(bf16[2,128,512]{2,1,0:T(8,128)(2,1)S(1)} %get-tuple-element.71), channel_id=1, source_target_pairs={{0,2},{1,3},{2,0},{3,1},{4,6},{5,7},{6,4},{7,5},{8,10},{9,11},{10,... | collective-permute-start | bytes 786440 | tf_op jit(solution)/shard_map/ppermute | solution.py:48
  65.4 15.1 %collective-permute-start.16 = (bf16[2,128,512]{2,1,0:T(8,128)(2,1)S(1)}, bf16[2,128,512]{2,1,0:T(8,128)(2,1)S(1)}, u32[]{:S(2)}, u32[]{:S(2)}) collective-permute-start(bf16[2,128,512]{2,1,0:T(8,128)(2,1)S(1)} %get-tuple-element.72), channel_id=1, source_target_pairs={{0,4},{1,5},{2,6},{3,7},{4,0},{5,1},{6,2},{7,3},{8,12},{9,13},{10,... | collective-permute-start | bytes 786440 | tf_op jit(solution)/shard_map/ppermute | solution.py:48
  68.7 11.8 %collective-permute-start.23 = (bf16[8,128,128]{2,1,0:T(8,128)(2,1)S(1)}, bf16[8,128,128]{2,1,0:T(8,128)(2,1)S(1)}, u32[]{:S(2)}, u32[]{:S(2)}) collective-permute-start(bf16[8,128,128]{2,1,0:T(8,128)(2,1)S(1)} %collective-permute-done.10.refs_12_), channel_id=1, source_target_pairs={{0,1},{1,0},{2,3},{3,2},{4,5},{5,4},{6,7},{7,6},{8,9},{9,8},{10,11... | collective-permute-start | bytes 786440 | tf_op jit(solution)/shard_map/ppermute | solution.py:48
  71.8 8.7 %collective-permute-start.24 = (bf16[8,128,128]{2,1,0:T(8,128)(2,1)S(1)}, bf16[8,128,128]{2,1,0:T(8,128)(2,1)S(1)}, u32[]{:S(2)}, u32[]{:S(2)}) collective-permute-start(bf16[8,128,128]{2,1,0:T(8,128)(2,1)S(1)} %collective-permute-done.11.refs_14_), channel_id=1, source_target_pairs={{0,1},{1,0},{2,3},{3,2},{4,5},{5,4},{6,7},{7,6},{8,9},{9,8},{10,11... | collective-permute-start | bytes 786440 | tf_op jit(solution)/shard_map/ppermute | solution.py:48
  77.4 3.2 %collective-permute-start.25 = (bf16[8,128,128]{2,1,0:T(8,128)(2,1)S(1)}, bf16[8,128,128]{2,1,0:T(8,128)(2,1)S(1)}, u32[]{:S(2)}, u32[]{:S(2)}) collective-permute-start(bf16[8,128,128]{2,1,0:T(8,128)(2,1)S(1)} %collective-permute-done.12.refs_16_), channel_id=1, source_target_pairs={{0,1},{1,0},{2,3},{3,2},{4,5},{5,4},{6,7},{7,6},{8,9},{9,8},{10,11... | collective-permute-start | bytes 786440 | tf_op jit(solution)/shard_map/ppermute | solution.py:48
  80.5 45.8 %copy-start.6 = (f32[256,512]{1,0:T(8,128)S(1)}, f32[256,512]{1,0:T(8,128)}, u32[]{:S(2)}) copy-start(f32[256,512]{1,0:T(8,128)} %get-tuple-element.75.kinv) | copy-start | bytes 1572868
  80.5 45.8 %copy-start.8 = (f32[512]{0:T(512)S(1)}, f32[512]{0:T(512)}, u32[]{:S(2)}) copy-start(f32[512]{0:T(512)} %param.20) | copy-start | bytes 6148
  82.8 21.0 %collective-permute-start.26 = (bf16[2,2,128,512]{3,2,1,0:T(8,128)(2,1)S(1)}, bf16[2,2,128,512]{3,2,1,0:T(8,128)(2,1)S(1)}, u32[]{:S(2)}, u32[]{:S(2)}) collective-permute-start(bf16[2,2,128,512]{3,2,1,0:T(8,128)(2,1)S(1)} %get-tuple-element.93), channel_id=1, source_target_pairs={{0,64},{32,96},{64,0},{96,32},{128,192},{160,224},{192,128},{224,1... | collective-permute-start | bytes 1572872 | tf_op jit(solution)/shard_map/ppermute | solution.py:48
  84.5 25.2 %collective-permute-start.27 = (bf16[2,2,128,512]{3,2,1,0:T(8,128)(2,1)S(1)}, bf16[2,2,128,512]{3,2,1,0:T(8,128)(2,1)S(1)}, u32[]{:S(2)}, u32[]{:S(2)}) collective-permute-start(bf16[2,2,128,512]{3,2,1,0:T(8,128)(2,1)S(1)} %get-tuple-element.94), channel_id=1, source_target_pairs={{0,128},{32,160},{64,192},{96,224},{128,0},{160,32},{192,64},{224,... | collective-permute-start | bytes 1572872 | tf_op jit(solution)/shard_map/ppermute | solution.py:48
  87.4 24.9 %collective-permute-start.28 = (bf16[2,2,128,512]{3,2,1,0:T(8,128)(2,1)S(1)}, bf16[2,2,128,512]{3,2,1,0:T(8,128)(2,1)S(1)}, u32[]{:S(2)}, u32[]{:S(2)}) collective-permute-start(bf16[2,2,128,512]{3,2,1,0:T(8,128)(2,1)S(1)} %get-tuple-element.95), channel_id=1, source_target_pairs={{0,192},{32,224},{64,128},{96,160},{128,64},{160,96},{192,0},{224,... | collective-permute-start | bytes 1572872 | tf_op jit(solution)/shard_map/ppermute | solution.py:48
  87.6 12.4 %collective-permute-start.17 = (bf16[2,128,512]{2,1,0:T(8,128)(2,1)S(1)}, bf16[2,128,512]{2,1,0:T(8,128)(2,1)S(1)}, u32[]{:S(2)}, u32[]{:S(2)}) collective-permute-start(bf16[2,128,512]{2,1,0:T(8,128)(2,1)S(1)} %get-tuple-element.73), channel_id=1, source_target_pairs={{0,6},{1,7},{2,4},{3,5},{4,2},{5,3},{6,0},{7,1},{8,14},{9,15},{10,... | collective-permute-start | bytes 786440 | tf_op jit(solution)/shard_map/ppermute | solution.py:48
  100.2 19.1 %collective-permute-start.20 = (bf16[256,1024]{1,0:T(8,128)(2,1)S(1)}, bf16[256,1024]{1,0:T(8,128)(2,1)S(1)}, u32[]{:S(2)}, u32[]{:S(2)}) collective-permute-start(bf16[256,1024]{1,0:T(8,128)(2,1)S(1)} %get-tuple-element.85), channel_id=1, source_target_pairs={{0,16},{8,24},{16,0},{24,8},{1,17},{9,25},{17,1},{25,9},{2,18},{10... | collective-permute-start | bytes 1572872 | tf_op jit(solution)/shard_map/ppermute | solution.py:48
  102.6 23.7 %collective-permute-start.19 = (bf16[256,1024]{1,0:T(8,128)(2,1)S(1)}, bf16[256,1024]{1,0:T(8,128)(2,1)S(1)}, u32[]{:S(2)}, u32[]{:S(2)}) collective-permute-start(bf16[256,1024]{1,0:T(8,128)(2,1)S(1)} %get-tuple-element.83), channel_id=1, source_target_pairs={{0,24},{8,16},{16,8},{24,0},{1,25},{9,17},{17,9},{25,1},{2,26},{10... | collective-permute-start | bytes 1572872 | tf_op jit(solution)/shard_map/ppermute | solution.py:48
  103.8 22.4 %collective-permute-start.18 = (bf16[256,1024]{1,0:T(8,128)(2,1)S(1)}, bf16[256,1024]{1,0:T(8,128)(2,1)S(1)}, u32[]{:S(2)}, u32[]{:S(2)}) collective-permute-start(bf16[256,1024]{1,0:T(8,128)(2,1)S(1)} %get-tuple-element.81), channel_id=1, source_target_pairs={{0,8},{8,0},{16,24},{24,16},{1,9},{9,1},{17,25},{25,17},{2,10},{10... | collective-permute-start | bytes 1572872 | tf_op jit(solution)/shard_map/ppermute | solution.py:48
  112.6 15.4 %collective-permute-start.29 = (bf16[2,128,512]{2,1,0:T(8,128)(2,1)S(1)}, bf16[2,128,512]{2,1,0:T(8,128)(2,1)S(1)}, u32[]{:S(2)}, u32[]{:S(2)}) collective-permute-start(bf16[2,128,512]{2,1,0:T(8,128)(2,1)S(1)} %fusion.1), channel_id=1, source_target_pairs={{0,32},{32,0},{64,96},{96,64},{128,160},{160,128},{192,224},{224,1... | collective-permute-start | bytes 786440 | tf_op jit(solution)/shard_map/ppermute | solution.py:48
  (11 other events, 94.0 us)

commit v2 on v1

--- a/solution.py
+++ b/solution.py
@@ -91,8 +91,12 @@
         copy.wait()
 
 
+def touch_kernel(w, out):
+    out[...] = w[:16, :LANES]
+
+
 def query_kernel(place, w, *refs):
-    x, out = refs[:8], refs[8]
+    x, out = refs[:8], refs[9]
     t = place[1]
     width = x[0].shape[2]
     total = None
@@ -240,6 +244,11 @@
         values[:, at] = dv.astype(BF)
 
 
+def last_kernel(near, far, query_out, output_out):
+    query_out[...] = near[0] + far[0].astype(F32)
+    output_out[...] = jnp.transpose(near[1] + far[1].astype(F32))
+
+
 def share(x):
     return [x] + [send(x, "seq", k) for k in range(1, 4)]
 
@@ -276,11 +285,13 @@
         left=4,
         vmem=60 * MIB,
     )(keys[0], values[0], rows[0], cotangent[0], kgain)
-    kv = share(message)
-    even = [own_block] + [send(after(own_block, kv[3]) if i == 1 else own_block, "tensor", 2 * i) for i in range(1, 4)]
-    even = [even[0], even[1], *after(even[2:], kv[1:3])]
+    even = [own_block] + [send(own_block, "tensor", 2 * i) for i in range(1, 4)]
+    touched = call(touch_kernel, [((16, LANES), BF)], smem=0)(w_query)[0]
+    kv = [message, send(message, "seq", 1), send(message, "seq", 3)]
+    kv.insert(2, send(after(message, (kv[1:], touched)), "seq", 2))
+    even = [even[0], even[1], *after(even[2:], (kv[1], kv[3]))]
     blocks = [b for e in even for b in (e, send(e, "tensor", 1))]
-    query = call(query_kernel, [(line, F32)])(place, w_query, *blocks)[0]
+    query = call(query_kernel, [(line, F32)])(place, w_query, *blocks, touched)[0]
     grad = call(gradient_kernel, [(line, BF)])(place, w_output, *blocks)[0]
     cut = call(cut_kernel, [((8, LANES, tokens), BF)] * 3)(place, *even)
     cut = [send(tile, "seq", k + 1) for k, tile in enumerate(cut)]
@@ -304,20 +315,25 @@
     )
 
     keep, other = call(product_kernel, [((2, 4, tokens, width), BF)] * 2)(
-        place, w_output, w_query, after(both, cut)
-    )
-    got = send(after(other, parts[1]), "tensor", 1)
+        place, w_output, w_query, after(both, (cut, kv_parts))
+    )
+    got = send(after(other, parts), "tensor", 1)
     pairs = call(pair_kernel, [((2, tokens, width), BF)] * 4, smem=0)(keep, got)
-    lines = [pairs[0]] + [send(pairs[i], "tensor", 2 * i) for i in range(1, 4)]
     sums = call(
         weight_kernel,
         [((2, 2, LANES, width), BF)] * 4,
         [pltpu.VMEM((4 * tokens, 2 * width), BF), pltpu.VMEM((2, 8 * LANES, 4 * tokens), BF)],
-    )(place, *blocks, *after(parts, (kv_parts, lines[1], lines[2])), *tiles)
-    sums = total_of([sums[0]] + [send(sums[m], "dp", 2 * m) for m in range(1, 4)])
-    lines = total_of(lines).astype(BF)
-    kv_sums = [kv_parts[0]] + [send(after(kv_parts[k], lines), "seq", k) for k in (1, 3, 2)]
-    weights = sums[0] + send(sums[1].astype(BF), "dp", 1).astype(F32)
+    )(place, *blocks, *after(parts, (kv_parts, pairs)), *tiles)
+    first = [send(sums[1], "dp", 2), send(sums[3], "dp", 6), send(after(kv_parts[1], sums), "seq", 1)]
+    first += [send(after(kv_parts[3], sums), "seq", 3), send(pairs[2], "tensor", 4)]
+    middle = after(sums[2], first[:4])
+    pairs, kv_parts = after((pairs, kv_parts), first)
+    lines = total_of([pairs[0], first[4], send(pairs[3], "tensor", 6), send(pairs[1], "tensor", 2)]).astype(BF)
+    sums = total_of([sums[0], first[0], first[1], send(middle, "dp", 4)])
+    kv_sums = [kv_parts[0], first[2], first[3], send(kv_parts[2], "seq", 2)]
+    query_weight_grad, output_weight_grad = call(
+        last_kernel, [((LANES, width), F32), ((width, LANES), F32)], smem=0
+    )(sums[0], send(sums[1].astype(BF), "dp", 1))
     keys_grad, values_grad = call(source_kernel, [((own, width), BF)] * 2, smem=0)(
         kgain, khat, kinv, *kv_sums
     )
@@ -326,8 +342,8 @@
         lines[1:],
         keys_grad[None],
         values_grad[None],
-        weights[0],
-        weights[1].T,
+        query_weight_grad,
+        output_weight_grad,
     )
 
 

time: 130 us -> 126 us (0.969)
  waiting for transfers between devices: 62.8 us -> 58.4 us
    ppermute x30, waiting for transfers between devices: 62.8 us -> 58.4 us  [send(): return lax.ppermute(x, axis, [(i, i ^ offset) for i in range(size)])]
    unnamed x27 -> x26, local copies, waits for them, and re-layouts: 4.18 us -> 5.35 us
    pallas_call x11 -> x13, Pallas kernels: 22.5 us -> 23.4 us  [run(): pl.pallas_call(kernel, out_shape=[jax.ShapeDtypeStruct(s, d) for s, d in...]
  transfers between devices with their start and end apart: 30 -> 30, of which waited for: 12 -> 19; matrix products, arithmetic and copies ran while one was open for 1% -> 1% of each run, Pallas kernels for 13% -> 13%
where the time goes in v2:
time: 126 us
  waiting for transfers between devices  58.4 us (46%)
  starting transfers between devices  36.8 us (29%)
  Pallas kernels  23.4 us (19%)
  local copies, waits for them, and re-layouts  6.13 us (5%)
    ppermute x30, waiting for transfers between devices, send(): return lax.ppermute(x, axis, [(i, i ^ offset) for i in range(size)])  58.4 us
    ppermute x30, starting transfers between devices, send(): return lax.ppermute(x, axis, [(i, i ^ offset) for i in range(size)])  36.8 us
    pallas_call x13, Pallas kernels, run(): pl.pallas_call(kernel, out_shape=[jax.ShapeDtypeStruct(s, d) for s, d in...  23.4 us
    unnamed x26, local copies, waits for them, and re-layouts  5.35 us
  transfers between devices with their start and end apart: 30, of which 19 were waited for; matrix products, arithmetic and copies ran while one was open for 1% of the time, Pallas kernels for 13%

profile of v2, /device:TPU:32, one launch (start us, length us, event | category | flops | bytes accessed | tf_op | source)
XLA Modules:
  0.0 126.0 jit_solution(8489606561007940252)
XLA Ops:
  0.6 3.8 %shard_map.154 = (bf16[2,128,512]{2,1,0:T(8,128)(2,1)}, bf16[256,1024]{1,0:T(8,128)(2,1)}, f32[256,512]{1,0:T(8,128)}, f32[256,512]{1,0:T(8,128)}) custom-call(bf16[256,512]{1,0:T(8,128)(2,1)} %bitcast.19, bf16[256,512]{1,0:T(8,128)(2,1)} %bitcast.20, bf16[128,512]{1,0:T(8,128)(2,1)} %bitcast.21, bf16[128,512]{1,0:T(8,128)(2,1)} %bitcast.22, f32[1,512]{1,0:T(1,128)} %bitcast.15), custom_call_target="tpu_custom_call" | custom-call | flops 1 | bytes 1 | tf_op jit(solution)/shard_map/pallas_call | solution.py:33
  6.0 2.1 %collective-permute-start.6 = (bf16[256,1024]{1,0:T(8,128)(2,1)}, bf16[256,1024]{1,0:T(8,128)(2,1)S(1)}, u32[]{:S(2)}, u32[]{:S(2)}) collective-permute-start(bf16[256,1024]{1,0:T(8,128)(2,1)} %get-tuple-element.62.refs_0_), channel_id=1, source_target_pairs={{0,24},{8,16},{16,8},{24,0},{1,25},{9,17},{17,9},{25,1},{2,26},{10... | collective-permute-start | bytes 1572872 | tf_op jit(solution)/shard_map/ppermute | solution.py:48
  8.2 3.3 %collective-permute-start.3 = (bf16[2,128,512]{2,1,0:T(8,128)(2,1)}, bf16[2,128,512]{2,1,0:T(8,128)(2,1)S(1)}, u32[]{:S(2)}, u32[]{:S(2)}) collective-permute-start(bf16[2,128,512]{2,1,0:T(8,128)(2,1)} %get-tuple-element.58.refs_0_), channel_id=1, source_target_pairs={{0,4},{1,5},{2,6},{3,7},{4,0},{5,1},{6,2},{7,3},{8,12},{9,13},{10,... | collective-permute-start | bytes 786440 | tf_op jit(solution)/shard_map/ppermute | solution.py:48
  11.9 2.2 %copy-done = bf16[4096,512]{1,0:T(8,128)(2,1)S(1)} copy-done((bf16[4096,512]{1,0:T(8,128)(2,1)S(1)}, bf16[4096,512]{1,0:T(8,128)(2,1)}, u32[]{:S(2)}) %copy-start) | copy-done | bytes 4194328
  14.1 4.3 %collective-permute-done.5.refs_1_ = bf16[256,1024]{1,0:T(8,128)(2,1)S(1)} collective-permute-done((bf16[256,1024]{1,0:T(8,128)(2,1)}, bf16[256,1024]{1,0:T(8,128)(2,1)S(1)}, u32[]{:S(2)}, u32[]{:S(2)}) %collective-permute-start.5) | collective-permute-done | bytes 524320 | tf_op jit(solution)/shard_map/ppermute | solution.py:48
  18.4 2.4 %collective-permute-done.6.refs_3_ = bf16[256,1024]{1,0:T(8,128)(2,1)S(1)} collective-permute-done((bf16[256,1024]{1,0:T(8,128)(2,1)}, bf16[256,1024]{1,0:T(8,128)(2,1)S(1)}, u32[]{:S(2)}, u32[]{:S(2)}) %collective-permute-start.6) | collective-permute-done | bytes 524320 | tf_op jit(solution)/shard_map/ppermute | solution.py:48
  22.8 6.9 %collective-permute-done.3.refs_4_.refs_2_ = bf16[2,128,512]{2,1,0:T(8,128)(2,1)S(1)} collective-permute-done((bf16[2,128,512]{2,1,0:T(8,128)(2,1)}, bf16[2,128,512]{2,1,0:T(8,128)(2,1)S(1)}, u32[]{:S(2)}, u32[]{:S(2)}) %collective-permute-start.3) | collective-permute-done | bytes 262176 | tf_op jit(solution)/shard_map/ppermute | solution.py:48
  29.8 4.7 %collective-permute-done.4.refs_6_.refs_3_ = bf16[2,128,512]{2,1,0:T(8,128)(2,1)S(1)} collective-permute-done((bf16[2,128,512]{2,1,0:T(8,128)(2,1)}, bf16[2,128,512]{2,1,0:T(8,128)(2,1)S(1)}, u32[]{:S(2)}, u32[]{:S(2)}) %collective-permute-start.4) | collective-permute-done | bytes 262176 | tf_op jit(solution)/shard_map/ppermute | solution.py:48
  36.6 2.0 %collective-permute-start.11 = (bf16[8,128,128]{2,1,0:T(8,128)(2,1)S(1)}, bf16[8,128,128]{2,1,0:T(8,128)(2,1)S(1)}, u32[]{:S(2)}, u32[]{:S(2)}) collective-permute-start(bf16[8,128,128]{2,1,0:T(8,128)(2,1)S(1)} %get-tuple-element.71), channel_id=1, source_target_pairs={{0,16},{8,24},{16,0},{24,8},{1,17},{9,25},{17,1},{25,9},{2,18},{10... | collective-permute-start | bytes 786440 | tf_op jit(solution)/shard_map/ppermute | solution.py:48
  38.6 2.1 %collective-permute-start.12 = (bf16[8,128,128]{2,1,0:T(8,128)(2,1)S(1)}, bf16[8,128,128]{2,1,0:T(8,128)(2,1)S(1)}, u32[]{:S(2)}, u32[]{:S(2)}) collective-permute-start(bf16[8,128,128]{2,1,0:T(8,128)(2,1)S(1)} %get-tuple-element.72), channel_id=1, source_target_pairs={{0,24},{8,16},{16,8},{24,0},{1,25},{9,17},{17,9},{25,1},{2,26},{10... | collective-permute-start | bytes 786440 | tf_op jit(solution)/shard_map/ppermute | solution.py:48
  40.7 2.2 %copy-done.1 = bf16[4096,512]{1,0:T(8,128)(2,1)S(1)} copy-done((bf16[4096,512]{1,0:T(8,128)(2,1)S(1)}, bf16[4096,512]{1,0:T(8,128)(2,1)}, u32[]{:S(2)}) %copy-start.1) | copy-done | bytes 4194328
  45.1 1.9 %shard_map.155.grad = bf16[128,512]{1,0:T(8,128)(2,1)S(1)} custom-call(s32[3]{0:T(128)S(1)} %pad_add_fusion.place, bf16[512,4096]{1,0:T(8,128)(2,1)S(1)} %copy-done.3, bf16[2,128,512]{2,1,0:T(8,128)(2,1)S(1)} %copy-done.4, bf16[2,128,512]{2,1,0:T(8,128)(2,1)S(1)} %collective-permute-done.refs_1_, ...), custom_call_target="tpu_custom_call" | custom-call | flops 1 | bytes 1 | tf_op jit(solution)/shard_map/pallas_call | solution.py:33
  47.0 4.8 %shard_map.158 = (bf16[128,512]{1,0:T(8,128)(2,1)S(1)}, f32[8,128,1024]{2,1,0:T(8,128)S(1)}, bf16[1024,512]{1,0:T(8,128)(2,1)S(1)}, bf16[1024,512]{1,0:T(8,128)(...) custom-call(s32[3]{0:T(128)S(1)} %pad_add_fusion.place, ...), custom_call_target="tpu_custom_call" | custom-call | flops 1 | bytes 1 | tf_op jit(solution)/shard_map/pallas_call | solution.py:33
  51.8 2.1 %shard_map.159 = (bf16[128,1024]{1,0:T(8,128)(2,1)S(1)}, bf16[8,128,1024]{2,1,0:T(8,128)(2,1)S(1)}) custom-call(f32[1,512]{1,0:T(1,128)S(1)} %bitcast.18, bf16[128,512]{1,0:T(8,128)(2,1)S(1)} %shard_map.155.grad, bf16[128,512]{1,0:T(8,128)(2,1)S(1)} %get-tuple-element.63.attended, f32[8,128,1024]{2,1,0:T(8,128)S(1)} %get-tuple-element.64.probs, ...), custom_call_target="tpu_custom_call" | custom-call | flops 1 | bytes 1 | tf_op jit(solution)/shard_map/pallas_call | solution.py:33
  54.0 2.6 %collective-permute-start.14 = (bf16[128,1024]{1,0:T(8,128)(2,1)S(1)}, bf16[128,1024]{1,0:T(8,128)(2,1)S(1)}, u32[]{:S(2)}, u32[]{:S(2)}) collective-permute-start(bf16[128,1024]{1,0:T(8,128)(2,1)S(1)} %get-tuple-element.88.both.refs_8_), channel_id=1, source_target_pairs={{0,16},{8,24},{16,0},{24,8},{1,17},{9,25},{17,1},{25,9},{2,18},{10... | collective-permute-start | bytes 786440 | tf_op jit(solution)/shard_map/ppermute | solution.py:48
  56.6 2.1 %collective-permute-start.15 = (bf16[128,1024]{1,0:T(8,128)(2,1)S(1)}, bf16[128,1024]{1,0:T(8,128)(2,1)S(1)}, u32[]{:S(2)}, u32[]{:S(2)}) collective-permute-start(bf16[128,1024]{1,0:T(8,128)(2,1)S(1)} %get-tuple-element.88.both.refs_8_), channel_id=1, source_target_pairs={{0,24},{8,16},{16,8},{24,0},{1,25},{9,17},{17,9},{25,1},{2,26},{10... | collective-permute-start | bytes 786440 | tf_op jit(solution)/shard_map/ppermute | solution.py:48
  60.0 2.5 %shard_map.162 = (bf16[2,4,128,512]{3,2,1,0:T(8,128)(2,1)S(1)}, bf16[2,4,128,512]{3,2,1,0:T(8,128)(2,1)S(1)}) custom-call(s32[3]{0:T(128)S(1)} %pad_add_fusion.place, bf16[512,4096]{1,0:T(8,128)(2,1)S(1)} %copy-done.3, bf16[4096,512]{1,0:T(8,128)(2,1)S(1)} %copy-done.2, bf16[128,1024]{1,0:T(8,128)(2,1)S(1)} %get-tuple-element.88.both.refs_8_), custom_call_target="tpu_custom_call" | custom-call | flops 1 | bytes 1 | tf_op jit(solution)/shard_map/pallas_call | solution.py:33
  63.2 4.4 %collective-permute-done.14.refs_10_ = bf16[128,1024]{1,0:T(8,128)(2,1)S(1)} collective-permute-done((bf16[128,1024]{1,0:T(8,128)(2,1)S(1)}, bf16[128,1024]{1,0:T(8,128)(2,1)S(1)}, u32[]{:S(2)}, u32[]{:S(2)}) %collective-permute-start.14) | collective-permute-done | bytes 262176 | tf_op jit(solution)/shard_map/ppermute | solution.py:48
  67.7 2.6 %collective-permute-done.15.refs_11_ = bf16[128,1024]{1,0:T(8,128)(2,1)S(1)} collective-permute-done((bf16[128,1024]{1,0:T(8,128)(2,1)S(1)}, bf16[128,1024]{1,0:T(8,128)(2,1)S(1)}, u32[]{:S(2)}, u32[]{:S(2)}) %collective-permute-start.15) | collective-permute-done | bytes 262176 | tf_op jit(solution)/shard_map/ppermute | solution.py:48
  71.3 1.6 %collective-permute-done.16.got = bf16[2,4,128,512]{3,2,1,0:T(8,128)(2,1)S(1)} collective-permute-done((bf16[2,4,128,512]{3,2,1,0:T(8,128)(2,1)S(1)}, bf16[2,4,128,512]{3,2,1,0:T(8,128)(2,1)S(1)}, u32[]{:S(2)}, u32[]{:S(2)}) %collective-permute-start.16) | collective-permute-done | bytes 1048608 | tf_op jit(solution)/shard_map/ppermute | solution.py:48
  74.0 2.3 %shard_map.164 = (bf16[2,2,128,512]{3,2,1,0:T(8,128)(2,1)S(1)}, bf16[2,2,128,512]{3,2,1,0:T(8,128)(2,1)S(1)}, bf16[2,2,128,512]{3,2,1,0:T(8,128)(2,1)S(1)}, bf16[2,2,128,512]{3,2,1,0:T(8,128)(2,1)S(1)}) custom-call(s32[3]{0:T(128)S(1)} %pad_add_fusion.place, bf16[2,128,512]{2,1,0:T(8,128)(2,1)S(1)} %copy-done.4, ...), custom_call_target="tpu_custom_call" | custom-call | flops 1 | bytes 1 | tf_op jit(solution)/shard_map/pallas_call | solution.py:33
  76.3 1.7 %collective-permute-start.20 = (bf16[2,2,128,512]{3,2,1,0:T(8,128)(2,1)S(1)}, bf16[2,2,128,512]{3,2,1,0:T(8,128)(2,1)S(1)}, u32[]{:S(2)}, u32[]{:S(2)}) collective-permute-start(bf16[2,2,128,512]{3,2,1,0:T(8,128)(2,1)S(1)} %get-tuple-element.92), channel_id=1, source_target_pairs={{0,64},{32,96},{64,0},{96,32},{128,192},{160,224},{192,128},{224,1... | collective-permute-start | bytes 1572872 | tf_op jit(solution)/shard_map/ppermute | solution.py:48
  78.0 2.2 %collective-permute-start.21 = (bf16[2,2,128,512]{3,2,1,0:T(8,128)(2,1)S(1)}, bf16[2,2,128,512]{3,2,1,0:T(8,128)(2,1)S(1)}, u32[]{:S(2)}, u32[]{:S(2)}) collective-permute-start(bf16[2,2,128,512]{3,2,1,0:T(8,128)(2,1)S(1)} %get-tuple-element.93), channel_id=1, source_target_pairs={{0,192},{32,224},{64,128},{96,160},{128,64},{160,96},{192,0},{224,... | collective-permute-start | bytes 1572872 | tf_op jit(solution)/shard_map/ppermute | solution.py:48
  80.1 2.1 %collective-permute-start.23 = (bf16[256,1024]{1,0:T(8,128)(2,1)S(1)}, bf16[256,1024]{1,0:T(8,128)(2,1)S(1)}, u32[]{:S(2)}, u32[]{:S(2)}) collective-permute-start(bf16[256,1024]{1,0:T(8,128)(2,1)S(1)} %get-tuple-element.97), channel_id=1, source_target_pairs={{0,24},{8,16},{16,8},{24,0},{1,25},{9,17},{17,9},{25,1},{2,26},{10... | collective-permute-start | bytes 1572872 | tf_op jit(solution)/shard_map/ppermute | solution.py:48
  82.2 8.1 %collective-permute-done.20 = bf16[2,2,128,512]{3,2,1,0:T(8,128)(2,1)S(1)} collective-permute-done((bf16[2,2,128,512]{3,2,1,0:T(8,128)(2,1)S(1)}, bf16[2,2,128,512]{3,2,1,0:T(8,128)(2,1)S(1)}, u32[]{:S(2)}, u32[]{:S(2)}) %collective-permute-start.20) | collective-permute-done | bytes 524320 | tf_op jit(solution)/shard_map/ppermute | solution.py:48
  90.3 2.5 %collective-permute-done.21 = bf16[2,2,128,512]{3,2,1,0:T(8,128)(2,1)S(1)} collective-permute-done((bf16[2,2,128,512]{3,2,1,0:T(8,128)(2,1)S(1)}, bf16[2,2,128,512]{3,2,1,0:T(8,128)(2,1)S(1)}, u32[]{:S(2)}, u32[]{:S(2)}) %collective-permute-start.21) | collective-permute-done | bytes 524320 | tf_op jit(solution)/shard_map/ppermute | solution.py:48
  97.2 2.1 %collective-permute-start.27 = (bf16[256,1024]{1,0:T(8,128)(2,1)S(1)}, bf16[256,1024]{1,0:T(8,128)(2,1)S(1)}, u32[]{:S(2)}, u32[]{:S(2)}) collective-permute-start(bf16[256,1024]{1,0:T(8,128)(2,1)S(1)} %get-tuple-element.104), channel_id=1, source_target_pairs={{0,16},{8,24},{16,0},{24,8},{1,17},{9,25},{17,1},{25,9},{2,18},{10... | collective-permute-start | bytes 1572872 | tf_op jit(solution)/shard_map/ppermute | solution.py:48
  99.3 5.7 %collective-permute-done.26 = bf16[2,128,512]{2,1,0:T(8,128)(2,1)S(1)} collective-permute-done((bf16[2,128,512]{2,1,0:T(8,128)(2,1)S(1)}, bf16[2,128,512]{2,1,0:T(8,128)(2,1)S(1)}, u32[]{:S(2)}, u32[]{:S(2)}) %collective-permute-start.26) | collective-permute-done | bytes 262176 | tf_op jit(solution)/shard_map/ppermute | solution.py:48
  105.3 3.4 %collective-permute-done.28 = bf16[2,2,128,512]{3,2,1,0:T(8,128)(2,1)S(1)} collective-permute-done((bf16[2,2,128,512]{3,2,1,0:T(8,128)(2,1)S(1)}, bf16[2,2,128,512]{3,2,1,0:T(8,128)(2,1)S(1)}, u32[]{:S(2)}, u32[]{:S(2)}) %collective-permute-start.28) | collective-permute-done | bytes 524320 | tf_op jit(solution)/shard_map/ppermute | solution.py:48
  109.0 5.7 %collective-permute-start.29 = (bf16[2,128,512]{2,1,0:T(8,128)(2,1)S(1)}, bf16[2,128,512]{2,1,0:T(8,128)(2,1)S(1)}, u32[]{:S(2)}, u32[]{:S(2)}) collective-permute-start(bf16[2,128,512]{2,1,0:T(8,128)(2,1)S(1)} %fusion), channel_id=1, source_target_pairs={{0,32},{32,0},{64,96},{96,64},{128,160},{160,128},{192,224},{224,1... | collective-permute-start | bytes 786440 | tf_op jit(solution)/shard_map/ppermute | solution.py:48
  115.5 1.7 %shard_map.165 = (bf16[256,512]{1,0:T(8,128)(2,1)}, bf16[256,512]{1,0:T(8,128)(2,1)}) custom-call(f32[1,512]{1,0:T(1,128)S(1)} %bitcast.16, f32[256,512]{1,0:T(8,128)S(1)} %copy-done.5, f32[256,512]{1,0:T(8,128)S(1)} %copy-done.6, bf16[256,1024]{1,0:T(8,128)(2,1)S(1)} %get-tuple-element.103.refs_0_, bf16[256,1024]{1,0:T(8,128)(2,1)S(1)} %collective-permute-done.22.refs_1_, ...), custom_call_target="tpu_custom_call" | custom-call | flops 1 | bytes 1 | tf_op jit(solution)/shard_map/pallas_call | solution.py:33
  117.2 7.9 %collective-permute-done.29.far = bf16[2,128,512]{2,1,0:T(8,128)(2,1)S(1)} collective-permute-done((bf16[2,128,512]{2,1,0:T(8,128)(2,1)S(1)}, bf16[2,128,512]{2,1,0:T(8,128)(2,1)S(1)}, u32[]{:S(2)}, u32[]{:S(2)}) %collective-permute-start.29) | collective-permute-done | bytes 262176 | tf_op jit(solution)/shard_map/ppermute | solution.py:48
  (73 shorter events, 19.3 us)
Async XLA Ops:
  4.4 14.0 %collective-permute-start.5 = (bf16[256,1024]{1,0:T(8,128)(2,1)}, bf16[256,1024]{1,0:T(8,128)(2,1)S(1)}, u32[]{:S(2)}, u32[]{:S(2)}) collective-permute-start(bf16[256,1024]{1,0:T(8,128)(2,1)} %get-tuple-element.62.refs_0_), channel_id=1, source_target_pairs={{0,8},{8,0},{16,24},{24,16},{1,9},{9,1},{17,25},{25,17},{2,10},{10... | collective-permute-start | bytes 1572872 | tf_op jit(solution)/shard_map/ppermute | solution.py:48
  6.0 14.8 %collective-permute-start.6 = (bf16[256,1024]{1,0:T(8,128)(2,1)}, bf16[256,1024]{1,0:T(8,128)(2,1)S(1)}, u32[]{:S(2)}, u32[]{:S(2)}) collective-permute-start(bf16[256,1024]{1,0:T(8,128)(2,1)} %get-tuple-element.62.refs_0_), channel_id=1, source_target_pairs={{0,24},{8,16},{16,8},{24,0},{1,25},{9,17},{17,9},{25,1},{2,26},{10... | collective-permute-start | bytes 1572872 | tf_op jit(solution)/shard_map/ppermute | solution.py:48
  8.1 14.2 %collective-permute-start.1 = (bf16[2,128,512]{2,1,0:T(8,128)(2,1)}, bf16[2,128,512]{2,1,0:T(8,128)(2,1)S(1)}, u32[]{:S(2)}, u32[]{:S(2)}) collective-permute-start(bf16[2,128,512]{2,1,0:T(8,128)(2,1)} %get-tuple-element.58.refs_0_), channel_id=1, source_target_pairs={{0,2},{1,3},{2,0},{3,1},{4,6},{5,7},{6,4},{7,5},{8,10},{9,11},{10,... | collective-permute-start | bytes 786440 | tf_op jit(solution)/shard_map/ppermute | solution.py:48
  8.2 21.6 %collective-permute-start.3 = (bf16[2,128,512]{2,1,0:T(8,128)(2,1)}, bf16[2,128,512]{2,1,0:T(8,128)(2,1)S(1)}, u32[]{:S(2)}, u32[]{:S(2)}) collective-permute-start(bf16[2,128,512]{2,1,0:T(8,128)(2,1)} %get-tuple-element.58.refs_0_), channel_id=1, source_target_pairs={{0,4},{1,5},{2,6},{3,7},{4,0},{5,1},{6,2},{7,3},{8,12},{9,13},{10,... | collective-permute-start | bytes 786440 | tf_op jit(solution)/shard_map/ppermute | solution.py:48
  11.5 23.1 %collective-permute-start.4 = (bf16[2,128,512]{2,1,0:T(8,128)(2,1)}, bf16[2,128,512]{2,1,0:T(8,128)(2,1)S(1)}, u32[]{:S(2)}, u32[]{:S(2)}) collective-permute-start(bf16[2,128,512]{2,1,0:T(8,128)(2,1)} %get-tuple-element.58.refs_0_), channel_id=1, source_target_pairs={{0,6},{1,7},{2,4},{3,5},{4,2},{5,3},{6,0},{7,1},{8,14},{9,15},{10,... | collective-permute-start | bytes 786440 | tf_op jit(solution)/shard_map/ppermute | solution.py:48
  20.8 26.2 %collective-permute-start.9 = (bf16[256,1024]{1,0:T(8,128)(2,1)S(1)}, bf16[256,1024]{1,0:T(8,128)(2,1)S(1)}, u32[]{:S(2)}, u32[]{:S(2)}) collective-permute-start(bf16[256,1024]{1,0:T(8,128)(2,1)S(1)} %copy-done.7), channel_id=1, source_target_pairs={{0,16},{8,24},{16,0},{24,8},{1,17},{9,25},{17,1},{25,9},{2,18},{10... | collective-permute-start | bytes 1572872 | tf_op jit(solution)/shard_map/ppermute | solution.py:48
  22.3 13.6 %collective-permute-start = (bf16[2,128,512]{2,1,0:T(8,128)(2,1)S(1)}, bf16[2,128,512]{2,1,0:T(8,128)(2,1)S(1)}, u32[]{:S(2)}, u32[]{:S(2)}) collective-permute-start(bf16[2,128,512]{2,1,0:T(8,128)(2,1)S(1)} %copy-done.4), channel_id=1, source_target_pairs={{0,1},{1,0},{2,3},{3,2},{4,5},{5,4},{6,7},{7,6},{8,9},{9,8},{10,11... | collective-permute-start | bytes 786440 | tf_op jit(solution)/shard_map/ppermute | solution.py:48
  22.3 14.3 %collective-permute-start.2 = (bf16[2,128,512]{2,1,0:T(8,128)(2,1)S(1)}, bf16[2,128,512]{2,1,0:T(8,128)(2,1)S(1)}, u32[]{:S(2)}, u32[]{:S(2)}) collective-permute-start(bf16[2,128,512]{2,1,0:T(8,128)(2,1)S(1)} %collective-permute-done.1.refs_2_.refs_1_), channel_id=1, source_target_pairs={{0,1},{1,0},{2,3},{3,2},{4,5},{5,4},{6,7},{7,6},{8,9},{9,8},{10,11... | collective-permute-start | bytes 786440 | tf_op jit(solution)/shard_map/ppermute | solution.py:48
  34.5 4.1 %collective-permute-start.7 = (bf16[2,128,512]{2,1,0:T(8,128)(2,1)S(1)}, bf16[2,128,512]{2,1,0:T(8,128)(2,1)S(1)}, u32[]{:S(2)}, u32[]{:S(2)}) collective-permute-start(bf16[2,128,512]{2,1,0:T(8,128)(2,1)S(1)} %collective-permute-done.3.refs_4_.refs_2_), channel_id=1, source_target_pairs={{0,1},{1,0},{2,3},{3,2},{4,5},{5,4},{6,7},{7,6},{8,9},{9,8},{10,11... | collective-permute-start | bytes 786440 | tf_op jit(solution)/shard_map/ppermute | solution.py:48
  34.5 6.2 %collective-permute-start.8 = (bf16[2,128,512]{2,1,0:T(8,128)(2,1)S(1)}, bf16[2,128,512]{2,1,0:T(8,128)(2,1)S(1)}, u32[]{:S(2)}, u32[]{:S(2)}) collective-permute-start(bf16[2,128,512]{2,1,0:T(8,128)(2,1)S(1)} %collective-permute-done.4.refs_6_.refs_3_), channel_id=1, source_target_pairs={{0,1},{1,0},{2,3},{3,2},{4,5},{5,4},{6,7},{7,6},{8,9},{9,8},{10,11... | collective-permute-start | bytes 786440 | tf_op jit(solution)/shard_map/ppermute | solution.py:48
  35.9 20.7 %collective-permute-start.10 = (bf16[8,128,128]{2,1,0:T(8,128)(2,1)S(1)}, bf16[8,128,128]{2,1,0:T(8,128)(2,1)S(1)}, u32[]{:S(2)}, u32[]{:S(2)}) collective-permute-start(bf16[8,128,128]{2,1,0:T(8,128)(2,1)S(1)} %get-tuple-element.70), channel_id=1, source_target_pairs={{0,8},{8,0},{16,24},{24,16},{1,9},{9,1},{17,25},{25,17},{2,10},{10... | collective-permute-start | bytes 786440 | tf_op jit(solution)/shard_map/ppermute | solution.py:48
  36.6 22.1 %collective-permute-start.11 = (bf16[8,128,128]{2,1,0:T(8,128)(2,1)S(1)}, bf16[8,128,128]{2,1,0:T(8,128)(2,1)S(1)}, u32[]{:S(2)}, u32[]{:S(2)}) collective-permute-start(bf16[8,128,128]{2,1,0:T(8,128)(2,1)S(1)} %get-tuple-element.71), channel_id=1, source_target_pairs={{0,16},{8,24},{16,0},{24,8},{1,17},{9,25},{17,1},{25,9},{2,18},{10... | collective-permute-start | bytes 786440 | tf_op jit(solution)/shard_map/ppermute | solution.py:48
  38.6 20.1 %collective-permute-start.12 = (bf16[8,128,128]{2,1,0:T(8,128)(2,1)S(1)}, bf16[8,128,128]{2,1,0:T(8,128)(2,1)S(1)}, u32[]{:S(2)}, u32[]{:S(2)}) collective-permute-start(bf16[8,128,128]{2,1,0:T(8,128)(2,1)S(1)} %get-tuple-element.72), channel_id=1, source_target_pairs={{0,24},{8,16},{16,8},{24,0},{1,25},{9,17},{17,9},{25,1},{2,26},{10... | collective-permute-start | bytes 786440 | tf_op jit(solution)/shard_map/ppermute | solution.py:48
  53.9 9.3 %collective-permute-start.13 = (bf16[128,1024]{1,0:T(8,128)(2,1)S(1)}, bf16[128,1024]{1,0:T(8,128)(2,1)S(1)}, u32[]{:S(2)}, u32[]{:S(2)}) collective-permute-start(bf16[128,1024]{1,0:T(8,128)(2,1)S(1)} %get-tuple-element.88.both.refs_8_), channel_id=1, source_target_pairs={{0,8},{8,0},{16,24},{24,16},{1,9},{9,1},{17,25},{25,17},{2,10},{10... | collective-permute-start | bytes 786440 | tf_op jit(solution)/shard_map/ppermute | solution.py:48
  54.0 13.7 %collective-permute-start.14 = (bf16[128,1024]{1,0:T(8,128)(2,1)S(1)}, bf16[128,1024]{1,0:T(8,128)(2,1)S(1)}, u32[]{:S(2)}, u32[]{:S(2)}) collective-permute-start(bf16[128,1024]{1,0:T(8,128)(2,1)S(1)} %get-tuple-element.88.both.refs_8_), channel_id=1, source_target_pairs={{0,16},{8,24},{16,0},{24,8},{1,17},{9,25},{17,1},{25,9},{2,18},{10... | collective-permute-start | bytes 786440 | tf_op jit(solution)/shard_map/ppermute | solution.py:48
  56.6 13.6 %collective-permute-start.15 = (bf16[128,1024]{1,0:T(8,128)(2,1)S(1)}, bf16[128,1024]{1,0:T(8,128)(2,1)S(1)}, u32[]{:S(2)}, u32[]{:S(2)}) collective-permute-start(bf16[128,1024]{1,0:T(8,128)(2,1)S(1)} %get-tuple-element.88.both.refs_8_), channel_id=1, source_target_pairs={{0,24},{8,16},{16,8},{24,0},{1,25},{9,17},{17,9},{25,1},{2,26},{10... | collective-permute-start | bytes 786440 | tf_op jit(solution)/shard_map/ppermute | solution.py:48
  70.2 2.7 %collective-permute-start.16 = (bf16[2,4,128,512]{3,2,1,0:T(8,128)(2,1)S(1)}, bf16[2,4,128,512]{3,2,1,0:T(8,128)(2,1)S(1)}, u32[]{:S(2)}, u32[]{:S(2)}) collective-permute-start(bf16[2,4,128,512]{3,2,1,0:T(8,128)(2,1)S(1)} %get-tuple-element.83), channel_id=1, source_target_pairs={{0,1},{1,0},{2,3},{3,2},{4,5},{5,4},{6,7},{7,6},{8,9},{9,8},{10,11... | collective-permute-start | bytes 3145736 | tf_op jit(solution)/shard_map/ppermute | solution.py:48
  70.2 3.0 %collective-permute-start.17 = (bf16[8,128,128]{2,1,0:T(8,128)(2,1)S(1)}, bf16[8,128,128]{2,1,0:T(8,128)(2,1)S(1)}, u32[]{:S(2)}, u32[]{:S(2)}) collective-permute-start(bf16[8,128,128]{2,1,0:T(8,128)(2,1)S(1)} %collective-permute-done.10.refs_12_), channel_id=1, source_target_pairs={{0,1},{1,0},{2,3},{3,2},{4,5},{5,4},{6,7},{7,6},{8,9},{9,8},{10,11... | collective-permute-start | bytes 786440 | tf_op jit(solution)/shard_map/ppermute | solution.py:48
  70.8 2.9 %collective-permute-start.18 = (bf16[8,128,128]{2,1,0:T(8,128)(2,1)S(1)}, bf16[8,128,128]{2,1,0:T(8,128)(2,1)S(1)}, u32[]{:S(2)}, u32[]{:S(2)}) collective-permute-start(bf16[8,128,128]{2,1,0:T(8,128)(2,1)S(1)} %collective-permute-done.11.refs_14_), channel_id=1, source_target_pairs={{0,1},{1,0},{2,3},{3,2},{4,5},{5,4},{6,7},{7,6},{8,9},{9,8},{10,11... | collective-permute-start | bytes 786440 | tf_op jit(solution)/shard_map/ppermute | solution.py:48
  70.8 3.3 %collective-permute-start.19 = (bf16[8,128,128]{2,1,0:T(8,128)(2,1)S(1)}, bf16[8,128,128]{2,1,0:T(8,128)(2,1)S(1)}, u32[]{:S(2)}, u32[]{:S(2)}) collective-permute-start(bf16[8,128,128]{2,1,0:T(8,128)(2,1)S(1)} %collective-permute-done.12.refs_16_), channel_id=1, source_target_pairs={{0,1},{1,0},{2,3},{3,2},{4,5},{5,4},{6,7},{7,6},{8,9},{9,8},{10,11... | collective-permute-start | bytes 786440 | tf_op jit(solution)/shard_map/ppermute | solution.py:48
  73.1 42.3 %copy-start.5 = (f32[256,512]{1,0:T(8,128)S(1)}, f32[256,512]{1,0:T(8,128)}, u32[]{:S(2)}) copy-start(f32[256,512]{1,0:T(8,128)} %get-tuple-element.101.khat) | copy-start | bytes 1572868
  73.2 42.3 %copy-start.6 = (f32[256,512]{1,0:T(8,128)S(1)}, f32[256,512]{1,0:T(8,128)}, u32[]{:S(2)}) copy-start(f32[256,512]{1,0:T(8,128)} %get-tuple-element.102.kinv) | copy-start | bytes 1572868
  76.3 14.0 %collective-permute-start.20 = (bf16[2,2,128,512]{3,2,1,0:T(8,128)(2,1)S(1)}, bf16[2,2,128,512]{3,2,1,0:T(8,128)(2,1)S(1)}, u32[]{:S(2)}, u32[]{:S(2)}) collective-permute-start(bf16[2,2,128,512]{3,2,1,0:T(8,128)(2,1)S(1)} %get-tuple-element.92), channel_id=1, source_target_pairs={{0,64},{32,96},{64,0},{96,32},{128,192},{160,224},{192,128},{224,1... | collective-permute-start | bytes 1572872 | tf_op jit(solution)/shard_map/ppermute | solution.py:48
  78.0 14.9 %collective-permute-start.21 = (bf16[2,2,128,512]{3,2,1,0:T(8,128)(2,1)S(1)}, bf16[2,2,128,512]{3,2,1,0:T(8,128)(2,1)S(1)}, u32[]{:S(2)}, u32[]{:S(2)}) collective-permute-start(bf16[2,2,128,512]{3,2,1,0:T(8,128)(2,1)S(1)} %get-tuple-element.93), channel_id=1, source_target_pairs={{0,192},{32,224},{64,128},{96,160},{128,64},{160,96},{192,0},{224,... | collective-permute-start | bytes 1572872 | tf_op jit(solution)/shard_map/ppermute | solution.py:48
  80.1 13.4 %collective-permute-start.22 = (bf16[256,1024]{1,0:T(8,128)(2,1)S(1)}, bf16[256,1024]{1,0:T(8,128)(2,1)S(1)}, u32[]{:S(2)}, u32[]{:S(2)}) collective-permute-start(bf16[256,1024]{1,0:T(8,128)(2,1)S(1)} %get-tuple-element.96), channel_id=1, source_target_pairs={{0,8},{8,0},{16,24},{24,16},{1,9},{9,1},{17,25},{25,17},{2,10},{10... | collective-permute-start | bytes 1572872 | tf_op jit(solution)/shard_map/ppermute | solution.py:48
  80.1 14.6 %collective-permute-start.23 = (bf16[256,1024]{1,0:T(8,128)(2,1)S(1)}, bf16[256,1024]{1,0:T(8,128)(2,1)S(1)}, u32[]{:S(2)}, u32[]{:S(2)}) collective-permute-start(bf16[256,1024]{1,0:T(8,128)(2,1)S(1)} %get-tuple-element.97), channel_id=1, source_target_pairs={{0,24},{8,16},{16,8},{24,0},{1,25},{9,17},{17,9},{25,1},{2,26},{10... | collective-permute-start | bytes 1572872 | tf_op jit(solution)/shard_map/ppermute | solution.py:48
  82.2 13.5 %collective-permute-start.24 = (bf16[2,128,512]{2,1,0:T(8,128)(2,1)S(1)}, bf16[2,128,512]{2,1,0:T(8,128)(2,1)S(1)}, u32[]{:S(2)}, u32[]{:S(2)}) collective-permute-start(bf16[2,128,512]{2,1,0:T(8,128)(2,1)S(1)} %get-tuple-element.86), channel_id=1, source_target_pairs={{0,4},{1,5},{2,6},{3,7},{4,0},{5,1},{6,2},{7,3},{8,12},{9,13},{10,... | collective-permute-start | bytes 786440 | tf_op jit(solution)/shard_map/ppermute | solution.py:48
  94.8 14.0 %collective-permute-start.28 = (bf16[2,2,128,512]{3,2,1,0:T(8,128)(2,1)S(1)}, bf16[2,2,128,512]{3,2,1,0:T(8,128)(2,1)S(1)}, u32[]{:S(2)}, u32[]{:S(2)}) collective-permute-start(bf16[2,2,128,512]{3,2,1,0:T(8,128)(2,1)S(1)} %get-tuple-element.107), channel_id=1, source_target_pairs={{0,128},{32,160},{64,192},{96,224},{128,0},{160,32},{192,64},{224,... | collective-permute-start | bytes 1572872 | tf_op jit(solution)/shard_map/ppermute | solution.py:48
  95.8 9.2 %collective-permute-start.26 = (bf16[2,128,512]{2,1,0:T(8,128)(2,1)S(1)}, bf16[2,128,512]{2,1,0:T(8,128)(2,1)S(1)}, u32[]{:S(2)}, u32[]{:S(2)}) collective-permute-start(bf16[2,128,512]{2,1,0:T(8,128)(2,1)S(1)} %get-tuple-element.100), channel_id=1, source_target_pairs={{0,2},{1,3},{2,0},{3,1},{4,6},{5,7},{6,4},{7,5},{8,10},{9,11},{10,... | collective-permute-start | bytes 786440 | tf_op jit(solution)/shard_map/ppermute | solution.py:48
  96.5 8.7 %collective-permute-start.25 = (bf16[2,128,512]{2,1,0:T(8,128)(2,1)S(1)}, bf16[2,128,512]{2,1,0:T(8,128)(2,1)S(1)}, u32[]{:S(2)}, u32[]{:S(2)}) collective-permute-start(bf16[2,128,512]{2,1,0:T(8,128)(2,1)S(1)} %get-tuple-element.99), channel_id=1, source_target_pairs={{0,6},{1,7},{2,4},{3,5},{4,2},{5,3},{6,0},{7,1},{8,14},{9,15},{10,... | collective-permute-start | bytes 786440 | tf_op jit(solution)/shard_map/ppermute | solution.py:48
  97.2 18.3 %collective-permute-start.27 = (bf16[256,1024]{1,0:T(8,128)(2,1)S(1)}, bf16[256,1024]{1,0:T(8,128)(2,1)S(1)}, u32[]{:S(2)}, u32[]{:S(2)}) collective-permute-start(bf16[256,1024]{1,0:T(8,128)(2,1)S(1)} %get-tuple-element.104), channel_id=1, source_target_pairs={{0,16},{8,24},{16,0},{24,8},{1,17},{9,25},{17,1},{25,9},{2,18},{10... | collective-permute-start | bytes 1572872 | tf_op jit(solution)/shard_map/ppermute | solution.py:48
  109.0 16.1 %collective-permute-start.29 = (bf16[2,128,512]{2,1,0:T(8,128)(2,1)S(1)}, bf16[2,128,512]{2,1,0:T(8,128)(2,1)S(1)}, u32[]{:S(2)}, u32[]{:S(2)}) collective-permute-start(bf16[2,128,512]{2,1,0:T(8,128)(2,1)S(1)} %fusion), channel_id=1, source_target_pairs={{0,32},{32,0},{64,96},{96,64},{128,160},{160,128},{192,224},{224,1... | collective-permute-start | bytes 786440 | tf_op jit(solution)/shard_map/ppermute | solution.py:48
  (11 other events, 77.5 us)

commit v3 on v2

--- a/solution.py
+++ b/solution.py
@@ -324,13 +324,13 @@
         [((2, 2, LANES, width), BF)] * 4,
         [pltpu.VMEM((4 * tokens, 2 * width), BF), pltpu.VMEM((2, 8 * LANES, 4 * tokens), BF)],
     )(place, *blocks, *after(parts, (kv_parts, pairs)), *tiles)
-    first = [send(sums[1], "dp", 2), send(sums[3], "dp", 6), send(after(kv_parts[1], sums), "seq", 1)]
-    first += [send(after(kv_parts[3], sums), "seq", 3), send(pairs[2], "tensor", 4)]
-    middle = after(sums[2], first[:4])
+    first = [send(sums[1], "dp", 2), send(sums[3], "dp", 6), send(pairs[2], "tensor", 4)]
+    first += [send(pairs[1], "tensor", 2), send(after(kv_parts[1], sums), "seq", 1)]
+    middle, third = after((sums[2], kv_parts[3]), first[:2])
     pairs, kv_parts = after((pairs, kv_parts), first)
-    lines = total_of([pairs[0], first[4], send(pairs[3], "tensor", 6), send(pairs[1], "tensor", 2)]).astype(BF)
+    lines = total_of([pairs[0], first[2], first[3], send(pairs[3], "tensor", 6)]).astype(BF)
     sums = total_of([sums[0], first[0], first[1], send(middle, "dp", 4)])
-    kv_sums = [kv_parts[0], first[2], first[3], send(kv_parts[2], "seq", 2)]
+    kv_sums = [kv_parts[0], first[4], send(third, "seq", 3), send(kv_parts[2], "seq", 2)]
     query_weight_grad, output_weight_grad = call(
         last_kernel, [((LANES, width), F32), ((width, LANES), F32)], smem=0
     )(sums[0], send(sums[1].astype(BF), "dp", 1))

time: 126 us -> 126 us (level)
  waiting for transfers between devices: 58.4 us -> 50.4 us
  starting transfers between devices: 36.8 us -> 44.7 us
    ppermute x30, waiting for transfers between devices: 58.4 us -> 50.4 us  [send(): return lax.ppermute(x, axis, [(i, i ^ offset) for i in range(size)])]
    ppermute x30, starting transfers between devices: 36.8 us -> 44.7 us  [send(): return lax.ppermute(x, axis, [(i, i ^ offset) for i in range(size)])]
  transfers between devices with their start and end apart: 30 -> 30, of which waited for: 19 -> 16; matrix products, arithmetic and copies ran while one was open for 1% -> 1% of each run, Pallas kernels for 13% -> 13%
where the time goes in v3:
time: 126 us
  waiting for transfers between devices  50.4 us (40%)
  starting transfers between devices  44.7 us (35%)
  Pallas kernels  23.4 us (19%)
  local copies, waits for them, and re-layouts  6.13 us (5%)
    ppermute x30, waiting for transfers between devices, send(): return lax.ppermute(x, axis, [(i, i ^ offset) for i in range(size)])  50.4 us
    ppermute x30, starting transfers between devices, send(): return lax.ppermute(x, axis, [(i, i ^ offset) for i in range(size)])  44.7 us
    pallas_call x13, Pallas kernels, run(): pl.pallas_call(kernel, out_shape=[jax.ShapeDtypeStruct(s, d) for s, d in...  23.4 us
    unnamed x26, local copies, waits for them, and re-layouts  5.35 us
  transfers between devices with their start and end apart: 30, of which 16 were waited for; matrix products, arithmetic and copies ran while one was open for 1% of the time, Pallas kernels for 13%

profile of v3, /device:TPU:32, one launch (start us, length us, event | category | flops | bytes accessed | tf_op | source)
XLA Modules:
  0.0 125.9 jit_solution(15704459943200971870)
XLA Ops:
  0.6 3.8 %shard_map.154 = (bf16[2,128,512]{2,1,0:T(8,128)(2,1)}, bf16[256,1024]{1,0:T(8,128)(2,1)}, f32[256,512]{1,0:T(8,128)}, f32[256,512]{1,0:T(8,128)}) custom-call(bf16[256,512]{1,0:T(8,128)(2,1)} %bitcast.19, bf16[256,512]{1,0:T(8,128)(2,1)} %bitcast.20, bf16[128,512]{1,0:T(8,128)(2,1)} %bitcast.21, bf16[128,512]{1,0:T(8,128)(2,1)} %bitcast.22, f32[1,512]{1,0:T(1,128)} %bitcast.15), custom_call_target="tpu_custom_call" | custom-call | flops 1 | bytes 1 | tf_op jit(solution)/shard_map/pallas_call | solution.py:33
  6.0 2.1 %collective-permute-start.6 = (bf16[256,1024]{1,0:T(8,128)(2,1)}, bf16[256,1024]{1,0:T(8,128)(2,1)S(1)}, u32[]{:S(2)}, u32[]{:S(2)}) collective-permute-start(bf16[256,1024]{1,0:T(8,128)(2,1)} %get-tuple-element.61.refs_0_), channel_id=1, source_target_pairs={{0,24},{8,16},{16,8},{24,0},{1,25},{9,17},{17,9},{25,1},{2,26},{10... | collective-permute-start | bytes 1572872 | tf_op jit(solution)/shard_map/ppermute | solution.py:48
  8.2 3.3 %collective-permute-start.3 = (bf16[2,128,512]{2,1,0:T(8,128)(2,1)}, bf16[2,128,512]{2,1,0:T(8,128)(2,1)S(1)}, u32[]{:S(2)}, u32[]{:S(2)}) collective-permute-start(bf16[2,128,512]{2,1,0:T(8,128)(2,1)} %get-tuple-element.57.refs_0_), channel_id=1, source_target_pairs={{0,4},{1,5},{2,6},{3,7},{4,0},{5,1},{6,2},{7,3},{8,12},{9,13},{10,... | collective-permute-start | bytes 786440 | tf_op jit(solution)/shard_map/ppermute | solution.py:48
  11.9 2.2 %copy-done = bf16[4096,512]{1,0:T(8,128)(2,1)S(1)} copy-done((bf16[4096,512]{1,0:T(8,128)(2,1)S(1)}, bf16[4096,512]{1,0:T(8,128)(2,1)}, u32[]{:S(2)}) %copy-start) | copy-done | bytes 4194328
  14.1 4.3 %collective-permute-done.5.refs_1_ = bf16[256,1024]{1,0:T(8,128)(2,1)S(1)} collective-permute-done((bf16[256,1024]{1,0:T(8,128)(2,1)}, bf16[256,1024]{1,0:T(8,128)(2,1)S(1)}, u32[]{:S(2)}, u32[]{:S(2)}) %collective-permute-start.5) | collective-permute-done | bytes 524320 | tf_op jit(solution)/shard_map/ppermute | solution.py:48
  18.4 2.4 %collective-permute-done.6.refs_3_ = bf16[256,1024]{1,0:T(8,128)(2,1)S(1)} collective-permute-done((bf16[256,1024]{1,0:T(8,128)(2,1)}, bf16[256,1024]{1,0:T(8,128)(2,1)S(1)}, u32[]{:S(2)}, u32[]{:S(2)}) %collective-permute-start.6) | collective-permute-done | bytes 524320 | tf_op jit(solution)/shard_map/ppermute | solution.py:48
  22.8 6.9 %collective-permute-done.3.refs_4_.refs_2_ = bf16[2,128,512]{2,1,0:T(8,128)(2,1)S(1)} collective-permute-done((bf16[2,128,512]{2,1,0:T(8,128)(2,1)}, bf16[2,128,512]{2,1,0:T(8,128)(2,1)S(1)}, u32[]{:S(2)}, u32[]{:S(2)}) %collective-permute-start.3) | collective-permute-done | bytes 262176 | tf_op jit(solution)/shard_map/ppermute | solution.py:48
  29.8 4.7 %collective-permute-done.4.refs_6_.refs_3_ = bf16[2,128,512]{2,1,0:T(8,128)(2,1)S(1)} collective-permute-done((bf16[2,128,512]{2,1,0:T(8,128)(2,1)}, bf16[2,128,512]{2,1,0:T(8,128)(2,1)S(1)}, u32[]{:S(2)}, u32[]{:S(2)}) %collective-permute-start.4) | collective-permute-done | bytes 262176 | tf_op jit(solution)/shard_map/ppermute | solution.py:48
  36.6 2.0 %collective-permute-start.11 = (bf16[8,128,128]{2,1,0:T(8,128)(2,1)S(1)}, bf16[8,128,128]{2,1,0:T(8,128)(2,1)S(1)}, u32[]{:S(2)}, u32[]{:S(2)}) collective-permute-start(bf16[8,128,128]{2,1,0:T(8,128)(2,1)S(1)} %get-tuple-element.70), channel_id=1, source_target_pairs={{0,16},{8,24},{16,0},{24,8},{1,17},{9,25},{17,1},{25,9},{2,18},{10... | collective-permute-start | bytes 786440 | tf_op jit(solution)/shard_map/ppermute | solution.py:48
  38.6 2.1 %collective-permute-start.12 = (bf16[8,128,128]{2,1,0:T(8,128)(2,1)S(1)}, bf16[8,128,128]{2,1,0:T(8,128)(2,1)S(1)}, u32[]{:S(2)}, u32[]{:S(2)}) collective-permute-start(bf16[8,128,128]{2,1,0:T(8,128)(2,1)S(1)} %get-tuple-element.71), channel_id=1, source_target_pairs={{0,24},{8,16},{16,8},{24,0},{1,25},{9,17},{17,9},{25,1},{2,26},{10... | collective-permute-start | bytes 786440 | tf_op jit(solution)/shard_map/ppermute | solution.py:48
  40.7 2.2 %copy-done.1 = bf16[4096,512]{1,0:T(8,128)(2,1)S(1)} copy-done((bf16[4096,512]{1,0:T(8,128)(2,1)S(1)}, bf16[4096,512]{1,0:T(8,128)(2,1)}, u32[]{:S(2)}) %copy-start.1) | copy-done | bytes 4194328
  45.1 1.9 %shard_map.155.grad = bf16[128,512]{1,0:T(8,128)(2,1)S(1)} custom-call(s32[3]{0:T(128)S(1)} %pad_add_fusion.place, bf16[512,4096]{1,0:T(8,128)(2,1)S(1)} %copy-done.3, bf16[2,128,512]{2,1,0:T(8,128)(2,1)S(1)} %copy-done.4, bf16[2,128,512]{2,1,0:T(8,128)(2,1)S(1)} %collective-permute-done.refs_1_, ...), custom_call_target="tpu_custom_call" | custom-call | flops 1 | bytes 1 | tf_op jit(solution)/shard_map/pallas_call | solution.py:33
  47.0 4.8 %shard_map.158 = (bf16[128,512]{1,0:T(8,128)(2,1)S(1)}, f32[8,128,1024]{2,1,0:T(8,128)S(1)}, bf16[1024,512]{1,0:T(8,128)(2,1)S(1)}, bf16[1024,512]{1,0:T(8,128)(...) custom-call(s32[3]{0:T(128)S(1)} %pad_add_fusion.place, ...), custom_call_target="tpu_custom_call" | custom-call | flops 1 | bytes 1 | tf_op jit(solution)/shard_map/pallas_call | solution.py:33
  51.8 2.1 %shard_map.159 = (bf16[128,1024]{1,0:T(8,128)(2,1)S(1)}, bf16[8,128,1024]{2,1,0:T(8,128)(2,1)S(1)}) custom-call(f32[1,512]{1,0:T(1,128)S(1)} %bitcast.18, bf16[128,512]{1,0:T(8,128)(2,1)S(1)} %shard_map.155.grad, bf16[128,512]{1,0:T(8,128)(2,1)S(1)} %get-tuple-element.62.attended, f32[8,128,1024]{2,1,0:T(8,128)S(1)} %get-tuple-element.63.probs, ...), custom_call_target="tpu_custom_call" | custom-call | flops 1 | bytes 1 | tf_op jit(solution)/shard_map/pallas_call | solution.py:33
  54.0 2.6 %collective-permute-start.14 = (bf16[128,1024]{1,0:T(8,128)(2,1)S(1)}, bf16[128,1024]{1,0:T(8,128)(2,1)S(1)}, u32[]{:S(2)}, u32[]{:S(2)}) collective-permute-start(bf16[128,1024]{1,0:T(8,128)(2,1)S(1)} %get-tuple-element.87.both.refs_8_), channel_id=1, source_target_pairs={{0,16},{8,24},{16,0},{24,8},{1,17},{9,25},{17,1},{25,9},{2,18},{10... | collective-permute-start | bytes 786440 | tf_op jit(solution)/shard_map/ppermute | solution.py:48
  56.6 2.1 %collective-permute-start.15 = (bf16[128,1024]{1,0:T(8,128)(2,1)S(1)}, bf16[128,1024]{1,0:T(8,128)(2,1)S(1)}, u32[]{:S(2)}, u32[]{:S(2)}) collective-permute-start(bf16[128,1024]{1,0:T(8,128)(2,1)S(1)} %get-tuple-element.87.both.refs_8_), channel_id=1, source_target_pairs={{0,24},{8,16},{16,8},{24,0},{1,25},{9,17},{17,9},{25,1},{2,26},{10... | collective-permute-start | bytes 786440 | tf_op jit(solution)/shard_map/ppermute | solution.py:48
  60.0 2.5 %shard_map.162 = (bf16[2,4,128,512]{3,2,1,0:T(8,128)(2,1)S(1)}, bf16[2,4,128,512]{3,2,1,0:T(8,128)(2,1)S(1)}) custom-call(s32[3]{0:T(128)S(1)} %pad_add_fusion.place, bf16[512,4096]{1,0:T(8,128)(2,1)S(1)} %copy-done.3, bf16[4096,512]{1,0:T(8,128)(2,1)S(1)} %copy-done.2, bf16[128,1024]{1,0:T(8,128)(2,1)S(1)} %get-tuple-element.87.both.refs_8_), custom_call_target="tpu_custom_call" | custom-call | flops 1 | bytes 1 | tf_op jit(solution)/shard_map/pallas_call | solution.py:33
  63.2 4.4 %collective-permute-done.14.refs_10_ = bf16[128,1024]{1,0:T(8,128)(2,1)S(1)} collective-permute-done((bf16[128,1024]{1,0:T(8,128)(2,1)S(1)}, bf16[128,1024]{1,0:T(8,128)(2,1)S(1)}, u32[]{:S(2)}, u32[]{:S(2)}) %collective-permute-start.14) | collective-permute-done | bytes 262176 | tf_op jit(solution)/shard_map/ppermute | solution.py:48
  67.7 2.6 %collective-permute-done.15.refs_11_ = bf16[128,1024]{1,0:T(8,128)(2,1)S(1)} collective-permute-done((bf16[128,1024]{1,0:T(8,128)(2,1)S(1)}, bf16[128,1024]{1,0:T(8,128)(2,1)S(1)}, u32[]{:S(2)}, u32[]{:S(2)}) %collective-permute-start.15) | collective-permute-done | bytes 262176 | tf_op jit(solution)/shard_map/ppermute | solution.py:48
  71.3 1.6 %collective-permute-done.16.got = bf16[2,4,128,512]{3,2,1,0:T(8,128)(2,1)S(1)} collective-permute-done((bf16[2,4,128,512]{3,2,1,0:T(8,128)(2,1)S(1)}, bf16[2,4,128,512]{3,2,1,0:T(8,128)(2,1)S(1)}, u32[]{:S(2)}, u32[]{:S(2)}) %collective-permute-start.16) | collective-permute-done | bytes 1048608 | tf_op jit(solution)/shard_map/ppermute | solution.py:48
  74.0 2.2 %shard_map.164 = (bf16[2,2,128,512]{3,2,1,0:T(8,128)(2,1)S(1)}, bf16[2,2,128,512]{3,2,1,0:T(8,128)(2,1)S(1)}, bf16[2,2,128,512]{3,2,1,0:T(8,128)(2,1)S(1)}, bf16[2,2,128,512]{3,2,1,0:T(8,128)(2,1)S(1)}) custom-call(s32[3]{0:T(128)S(1)} %pad_add_fusion.place, bf16[2,128,512]{2,1,0:T(8,128)(2,1)S(1)} %copy-done.4, ...), custom_call_target="tpu_custom_call" | custom-call | flops 1 | bytes 1 | tf_op jit(solution)/shard_map/pallas_call | solution.py:33
  76.3 1.7 %collective-permute-start.20 = (bf16[2,2,128,512]{3,2,1,0:T(8,128)(2,1)S(1)}, bf16[2,2,128,512]{3,2,1,0:T(8,128)(2,1)S(1)}, u32[]{:S(2)}, u32[]{:S(2)}) collective-permute-start(bf16[2,2,128,512]{3,2,1,0:T(8,128)(2,1)S(1)} %get-tuple-element.91), channel_id=1, source_target_pairs={{0,64},{32,96},{64,0},{96,32},{128,192},{160,224},{192,128},{224,1... | collective-permute-start | bytes 1572872 | tf_op jit(solution)/shard_map/ppermute | solution.py:48
  77.9 2.2 %collective-permute-start.21 = (bf16[2,2,128,512]{3,2,1,0:T(8,128)(2,1)S(1)}, bf16[2,2,128,512]{3,2,1,0:T(8,128)(2,1)S(1)}, u32[]{:S(2)}, u32[]{:S(2)}) collective-permute-start(bf16[2,2,128,512]{3,2,1,0:T(8,128)(2,1)S(1)} %get-tuple-element.92), channel_id=1, source_target_pairs={{0,192},{32,224},{64,128},{96,160},{128,64},{160,96},{192,0},{224,... | collective-permute-start | bytes 1572872 | tf_op jit(solution)/shard_map/ppermute | solution.py:48
  80.1 2.9 %collective-permute-start.23 = (bf16[2,128,512]{2,1,0:T(8,128)(2,1)S(1)}, bf16[2,128,512]{2,1,0:T(8,128)(2,1)S(1)}, u32[]{:S(2)}, u32[]{:S(2)}) collective-permute-start(bf16[2,128,512]{2,1,0:T(8,128)(2,1)S(1)} %get-tuple-element.84), channel_id=1, source_target_pairs={{0,2},{1,3},{2,0},{3,1},{4,6},{5,7},{6,4},{7,5},{8,10},{9,11},{10,... | collective-permute-start | bytes 786440 | tf_op jit(solution)/shard_map/ppermute | solution.py:48
  83.0 7.3 %collective-permute-done.20 = bf16[2,2,128,512]{3,2,1,0:T(8,128)(2,1)S(1)} collective-permute-done((bf16[2,2,128,512]{3,2,1,0:T(8,128)(2,1)S(1)}, bf16[2,2,128,512]{3,2,1,0:T(8,128)(2,1)S(1)}, u32[]{:S(2)}, u32[]{:S(2)}) %collective-permute-start.20) | collective-permute-done | bytes 524320 | tf_op jit(solution)/shard_map/ppermute | solution.py:48
  90.3 2.5 %collective-permute-done.21 = bf16[2,2,128,512]{3,2,1,0:T(8,128)(2,1)S(1)} collective-permute-done((bf16[2,2,128,512]{3,2,1,0:T(8,128)(2,1)S(1)}, bf16[2,2,128,512]{3,2,1,0:T(8,128)(2,1)S(1)}, u32[]{:S(2)}, u32[]{:S(2)}) %collective-permute-start.21) | collective-permute-done | bytes 524320 | tf_op jit(solution)/shard_map/ppermute | solution.py:48
  92.8 1.7 %collective-permute-start.28 = (bf16[2,2,128,512]{3,2,1,0:T(8,128)(2,1)S(1)}, bf16[2,2,128,512]{3,2,1,0:T(8,128)(2,1)S(1)}, u32[]{:S(2)}, u32[]{:S(2)}) collective-permute-start(bf16[2,2,128,512]{3,2,1,0:T(8,128)(2,1)S(1)} %get-tuple-element.105), channel_id=1, source_target_pairs={{0,128},{32,160},{64,192},{96,224},{128,0},{160,32},{192,64},{224,... | collective-permute-start | bytes 1572872 | tf_op jit(solution)/shard_map/ppermute | solution.py:48
  96.1 2.1 %collective-permute-start.26 = (bf16[256,1024]{1,0:T(8,128)(2,1)S(1)}, bf16[256,1024]{1,0:T(8,128)(2,1)S(1)}, u32[]{:S(2)}, u32[]{:S(2)}) collective-permute-start(bf16[256,1024]{1,0:T(8,128)(2,1)S(1)} %get-tuple-element.101), channel_id=1, source_target_pairs={{0,24},{8,16},{16,8},{24,0},{1,25},{9,17},{17,9},{25,1},{2,26},{10... | collective-permute-start | bytes 1572872 | tf_op jit(solution)/shard_map/ppermute | solution.py:48
  98.9 8.3 %collective-permute-done.25 = bf16[2,128,512]{2,1,0:T(8,128)(2,1)S(1)} collective-permute-done((bf16[2,128,512]{2,1,0:T(8,128)(2,1)S(1)}, bf16[2,128,512]{2,1,0:T(8,128)(2,1)S(1)}, u32[]{:S(2)}, u32[]{:S(2)}) %collective-permute-start.25) | collective-permute-done | bytes 262176 | tf_op jit(solution)/shard_map/ppermute | solution.py:48
  107.6 11.3 %collective-permute-start.29 = (bf16[2,128,512]{2,1,0:T(8,128)(2,1)S(1)}, bf16[2,128,512]{2,1,0:T(8,128)(2,1)S(1)}, u32[]{:S(2)}, u32[]{:S(2)}) collective-permute-start(bf16[2,128,512]{2,1,0:T(8,128)(2,1)S(1)} %fusion), channel_id=1, source_target_pairs={{0,32},{32,0},{64,96},{96,64},{128,160},{160,128},{192,224},{224,1... | collective-permute-start | bytes 786440 | tf_op jit(solution)/shard_map/ppermute | solution.py:48
  120.8 1.7 %shard_map.165 = (bf16[256,512]{1,0:T(8,128)(2,1)}, bf16[256,512]{1,0:T(8,128)(2,1)}) custom-call(f32[1,512]{1,0:T(1,128)S(1)} %bitcast.16, f32[256,512]{1,0:T(8,128)S(1)} %copy-done.5, f32[256,512]{1,0:T(8,128)S(1)} %copy-done.6, bf16[256,1024]{1,0:T(8,128)(2,1)S(1)} %get-tuple-element.100.refs_0_, bf16[256,1024]{1,0:T(8,128)(2,1)S(1)} %collective-permute-done.24.refs_1_, ...), custom_call_target="tpu_custom_call" | custom-call | flops 1 | bytes 1 | tf_op jit(solution)/shard_map/pallas_call | solution.py:33
  122.5 2.5 %collective-permute-done.29.far = bf16[2,128,512]{2,1,0:T(8,128)(2,1)S(1)} collective-permute-done((bf16[2,128,512]{2,1,0:T(8,128)(2,1)S(1)}, bf16[2,128,512]{2,1,0:T(8,128)(2,1)S(1)}, u32[]{:S(2)}, u32[]{:S(2)}) %collective-permute-start.29) | collective-permute-done | bytes 262176 | tf_op jit(solution)/shard_map/ppermute | solution.py:48
  (73 shorter events, 18.2 us)
Async XLA Ops:
  4.4 14.0 %collective-permute-start.5 = (bf16[256,1024]{1,0:T(8,128)(2,1)}, bf16[256,1024]{1,0:T(8,128)(2,1)S(1)}, u32[]{:S(2)}, u32[]{:S(2)}) collective-permute-start(bf16[256,1024]{1,0:T(8,128)(2,1)} %get-tuple-element.61.refs_0_), channel_id=1, source_target_pairs={{0,8},{8,0},{16,24},{24,16},{1,9},{9,1},{17,25},{25,17},{2,10},{10... | collective-permute-start | bytes 1572872 | tf_op jit(solution)/shard_map/ppermute | solution.py:48
  6.0 14.8 %collective-permute-start.6 = (bf16[256,1024]{1,0:T(8,128)(2,1)}, bf16[256,1024]{1,0:T(8,128)(2,1)S(1)}, u32[]{:S(2)}, u32[]{:S(2)}) collective-permute-start(bf16[256,1024]{1,0:T(8,128)(2,1)} %get-tuple-element.61.refs_0_), channel_id=1, source_target_pairs={{0,24},{8,16},{16,8},{24,0},{1,25},{9,17},{17,9},{25,1},{2,26},{10... | collective-permute-start | bytes 1572872 | tf_op jit(solution)/shard_map/ppermute | solution.py:48
  8.1 14.2 %collective-permute-start.1 = (bf16[2,128,512]{2,1,0:T(8,128)(2,1)}, bf16[2,128,512]{2,1,0:T(8,128)(2,1)S(1)}, u32[]{:S(2)}, u32[]{:S(2)}) collective-permute-start(bf16[2,128,512]{2,1,0:T(8,128)(2,1)} %get-tuple-element.57.refs_0_), channel_id=1, source_target_pairs={{0,2},{1,3},{2,0},{3,1},{4,6},{5,7},{6,4},{7,5},{8,10},{9,11},{10,... | collective-permute-start | bytes 786440 | tf_op jit(solution)/shard_map/ppermute | solution.py:48
  8.2 21.6 %collective-permute-start.3 = (bf16[2,128,512]{2,1,0:T(8,128)(2,1)}, bf16[2,128,512]{2,1,0:T(8,128)(2,1)S(1)}, u32[]{:S(2)}, u32[]{:S(2)}) collective-permute-start(bf16[2,128,512]{2,1,0:T(8,128)(2,1)} %get-tuple-element.57.refs_0_), channel_id=1, source_target_pairs={{0,4},{1,5},{2,6},{3,7},{4,0},{5,1},{6,2},{7,3},{8,12},{9,13},{10,... | collective-permute-start | bytes 786440 | tf_op jit(solution)/shard_map/ppermute | solution.py:48
  11.5 23.1 %collective-permute-start.4 = (bf16[2,128,512]{2,1,0:T(8,128)(2,1)}, bf16[2,128,512]{2,1,0:T(8,128)(2,1)S(1)}, u32[]{:S(2)}, u32[]{:S(2)}) collective-permute-start(bf16[2,128,512]{2,1,0:T(8,128)(2,1)} %get-tuple-element.57.refs_0_), channel_id=1, source_target_pairs={{0,6},{1,7},{2,4},{3,5},{4,2},{5,3},{6,0},{7,1},{8,14},{9,15},{10,... | collective-permute-start | bytes 786440 | tf_op jit(solution)/shard_map/ppermute | solution.py:48
  20.8 26.2 %collective-permute-start.9 = (bf16[256,1024]{1,0:T(8,128)(2,1)S(1)}, bf16[256,1024]{1,0:T(8,128)(2,1)S(1)}, u32[]{:S(2)}, u32[]{:S(2)}) collective-permute-start(bf16[256,1024]{1,0:T(8,128)(2,1)S(1)} %copy-done.7), channel_id=1, source_target_pairs={{0,16},{8,24},{16,0},{24,8},{1,17},{9,25},{17,1},{25,9},{2,18},{10... | collective-permute-start | bytes 1572872 | tf_op jit(solution)/shard_map/ppermute | solution.py:48
  22.3 13.6 %collective-permute-start = (bf16[2,128,512]{2,1,0:T(8,128)(2,1)S(1)}, bf16[2,128,512]{2,1,0:T(8,128)(2,1)S(1)}, u32[]{:S(2)}, u32[]{:S(2)}) collective-permute-start(bf16[2,128,512]{2,1,0:T(8,128)(2,1)S(1)} %copy-done.4), channel_id=1, source_target_pairs={{0,1},{1,0},{2,3},{3,2},{4,5},{5,4},{6,7},{7,6},{8,9},{9,8},{10,11... | collective-permute-start | bytes 786440 | tf_op jit(solution)/shard_map/ppermute | solution.py:48
  22.3 14.3 %collective-permute-start.2 = (bf16[2,128,512]{2,1,0:T(8,128)(2,1)S(1)}, bf16[2,128,512]{2,1,0:T(8,128)(2,1)S(1)}, u32[]{:S(2)}, u32[]{:S(2)}) collective-permute-start(bf16[2,128,512]{2,1,0:T(8,128)(2,1)S(1)} %collective-permute-done.1.refs_2_.refs_1_), channel_id=1, source_target_pairs={{0,1},{1,0},{2,3},{3,2},{4,5},{5,4},{6,7},{7,6},{8,9},{9,8},{10,11... | collective-permute-start | bytes 786440 | tf_op jit(solution)/shard_map/ppermute | solution.py:48
  34.5 4.1 %collective-permute-start.7 = (bf16[2,128,512]{2,1,0:T(8,128)(2,1)S(1)}, bf16[2,128,512]{2,1,0:T(8,128)(2,1)S(1)}, u32[]{:S(2)}, u32[]{:S(2)}) collective-permute-start(bf16[2,128,512]{2,1,0:T(8,128)(2,1)S(1)} %collective-permute-done.3.refs_4_.refs_2_), channel_id=1, source_target_pairs={{0,1},{1,0},{2,3},{3,2},{4,5},{5,4},{6,7},{7,6},{8,9},{9,8},{10,11... | collective-permute-start | bytes 786440 | tf_op jit(solution)/shard_map/ppermute | solution.py:48
  34.5 6.2 %collective-permute-start.8 = (bf16[2,128,512]{2,1,0:T(8,128)(2,1)S(1)}, bf16[2,128,512]{2,1,0:T(8,128)(2,1)S(1)}, u32[]{:S(2)}, u32[]{:S(2)}) collective-permute-start(bf16[2,128,512]{2,1,0:T(8,128)(2,1)S(1)} %collective-permute-done.4.refs_6_.refs_3_), channel_id=1, source_target_pairs={{0,1},{1,0},{2,3},{3,2},{4,5},{5,4},{6,7},{7,6},{8,9},{9,8},{10,11... | collective-permute-start | bytes 786440 | tf_op jit(solution)/shard_map/ppermute | solution.py:48
  35.9 20.7 %collective-permute-start.10 = (bf16[8,128,128]{2,1,0:T(8,128)(2,1)S(1)}, bf16[8,128,128]{2,1,0:T(8,128)(2,1)S(1)}, u32[]{:S(2)}, u32[]{:S(2)}) collective-permute-start(bf16[8,128,128]{2,1,0:T(8,128)(2,1)S(1)} %get-tuple-element.69), channel_id=1, source_target_pairs={{0,8},{8,0},{16,24},{24,16},{1,9},{9,1},{17,25},{25,17},{2,10},{10... | collective-permute-start | bytes 786440 | tf_op jit(solution)/shard_map/ppermute | solution.py:48
  36.6 22.1 %collective-permute-start.11 = (bf16[8,128,128]{2,1,0:T(8,128)(2,1)S(1)}, bf16[8,128,128]{2,1,0:T(8,128)(2,1)S(1)}, u32[]{:S(2)}, u32[]{:S(2)}) collective-permute-start(bf16[8,128,128]{2,1,0:T(8,128)(2,1)S(1)} %get-tuple-element.70), channel_id=1, source_target_pairs={{0,16},{8,24},{16,0},{24,8},{1,17},{9,25},{17,1},{25,9},{2,18},{10... | collective-permute-start | bytes 786440 | tf_op jit(solution)/shard_map/ppermute | solution.py:48
  38.6 20.1 %collective-permute-start.12 = (bf16[8,128,128]{2,1,0:T(8,128)(2,1)S(1)}, bf16[8,128,128]{2,1,0:T(8,128)(2,1)S(1)}, u32[]{:S(2)}, u32[]{:S(2)}) collective-permute-start(bf16[8,128,128]{2,1,0:T(8,128)(2,1)S(1)} %get-tuple-element.71), channel_id=1, source_target_pairs={{0,24},{8,16},{16,8},{24,0},{1,25},{9,17},{17,9},{25,1},{2,26},{10... | collective-permute-start | bytes 786440 | tf_op jit(solution)/shard_map/ppermute | solution.py:48
  53.9 9.3 %collective-permute-start.13 = (bf16[128,1024]{1,0:T(8,128)(2,1)S(1)}, bf16[128,1024]{1,0:T(8,128)(2,1)S(1)}, u32[]{:S(2)}, u32[]{:S(2)}) collective-permute-start(bf16[128,1024]{1,0:T(8,128)(2,1)S(1)} %get-tuple-element.87.both.refs_8_), channel_id=1, source_target_pairs={{0,8},{8,0},{16,24},{24,16},{1,9},{9,1},{17,25},{25,17},{2,10},{10... | collective-permute-start | bytes 786440 | tf_op jit(solution)/shard_map/ppermute | solution.py:48
  54.0 13.7 %collective-permute-start.14 = (bf16[128,1024]{1,0:T(8,128)(2,1)S(1)}, bf16[128,1024]{1,0:T(8,128)(2,1)S(1)}, u32[]{:S(2)}, u32[]{:S(2)}) collective-permute-start(bf16[128,1024]{1,0:T(8,128)(2,1)S(1)} %get-tuple-element.87.both.refs_8_), channel_id=1, source_target_pairs={{0,16},{8,24},{16,0},{24,8},{1,17},{9,25},{17,1},{25,9},{2,18},{10... | collective-permute-start | bytes 786440 | tf_op jit(solution)/shard_map/ppermute | solution.py:48
  56.6 13.6 %collective-permute-start.15 = (bf16[128,1024]{1,0:T(8,128)(2,1)S(1)}, bf16[128,1024]{1,0:T(8,128)(2,1)S(1)}, u32[]{:S(2)}, u32[]{:S(2)}) collective-permute-start(bf16[128,1024]{1,0:T(8,128)(2,1)S(1)} %get-tuple-element.87.both.refs_8_), channel_id=1, source_target_pairs={{0,24},{8,16},{16,8},{24,0},{1,25},{9,17},{17,9},{25,1},{2,26},{10... | collective-permute-start | bytes 786440 | tf_op jit(solution)/shard_map/ppermute | solution.py:48
  70.2 2.7 %collective-permute-start.16 = (bf16[2,4,128,512]{3,2,1,0:T(8,128)(2,1)S(1)}, bf16[2,4,128,512]{3,2,1,0:T(8,128)(2,1)S(1)}, u32[]{:S(2)}, u32[]{:S(2)}) collective-permute-start(bf16[2,4,128,512]{3,2,1,0:T(8,128)(2,1)S(1)} %get-tuple-element.82), channel_id=1, source_target_pairs={{0,1},{1,0},{2,3},{3,2},{4,5},{5,4},{6,7},{7,6},{8,9},{9,8},{10,11... | collective-permute-start | bytes 3145736 | tf_op jit(solution)/shard_map/ppermute | solution.py:48
  70.2 3.0 %collective-permute-start.17 = (bf16[8,128,128]{2,1,0:T(8,128)(2,1)S(1)}, bf16[8,128,128]{2,1,0:T(8,128)(2,1)S(1)}, u32[]{:S(2)}, u32[]{:S(2)}) collective-permute-start(bf16[8,128,128]{2,1,0:T(8,128)(2,1)S(1)} %collective-permute-done.10.refs_12_), channel_id=1, source_target_pairs={{0,1},{1,0},{2,3},{3,2},{4,5},{5,4},{6,7},{7,6},{8,9},{9,8},{10,11... | collective-permute-start | bytes 786440 | tf_op jit(solution)/shard_map/ppermute | solution.py:48
  70.8 2.9 %collective-permute-start.18 = (bf16[8,128,128]{2,1,0:T(8,128)(2,1)S(1)}, bf16[8,128,128]{2,1,0:T(8,128)(2,1)S(1)}, u32[]{:S(2)}, u32[]{:S(2)}) collective-permute-start(bf16[8,128,128]{2,1,0:T(8,128)(2,1)S(1)} %collective-permute-done.11.refs_14_), channel_id=1, source_target_pairs={{0,1},{1,0},{2,3},{3,2},{4,5},{5,4},{6,7},{7,6},{8,9},{9,8},{10,11... | collective-permute-start | bytes 786440 | tf_op jit(solution)/shard_map/ppermute | solution.py:48
  70.8 3.3 %collective-permute-start.19 = (bf16[8,128,128]{2,1,0:T(8,128)(2,1)S(1)}, bf16[8,128,128]{2,1,0:T(8,128)(2,1)S(1)}, u32[]{:S(2)}, u32[]{:S(2)}) collective-permute-start(bf16[8,128,128]{2,1,0:T(8,128)(2,1)S(1)} %collective-permute-done.12.refs_16_), channel_id=1, source_target_pairs={{0,1},{1,0},{2,3},{3,2},{4,5},{5,4},{6,7},{7,6},{8,9},{9,8},{10,11... | collective-permute-start | bytes 786440 | tf_op jit(solution)/shard_map/ppermute | solution.py:48
  73.1 47.6 %copy-start.5 = (f32[256,512]{1,0:T(8,128)S(1)}, f32[256,512]{1,0:T(8,128)}, u32[]{:S(2)}) copy-start(f32[256,512]{1,0:T(8,128)} %get-tuple-element.98.khat) | copy-start | bytes 1572868
  73.2 47.6 %copy-start.6 = (f32[256,512]{1,0:T(8,128)S(1)}, f32[256,512]{1,0:T(8,128)}, u32[]{:S(2)}) copy-start(f32[256,512]{1,0:T(8,128)} %get-tuple-element.99.kinv) | copy-start | bytes 1572868
  76.3 14.1 %collective-permute-start.20 = (bf16[2,2,128,512]{3,2,1,0:T(8,128)(2,1)S(1)}, bf16[2,2,128,512]{3,2,1,0:T(8,128)(2,1)S(1)}, u32[]{:S(2)}, u32[]{:S(2)}) collective-permute-start(bf16[2,2,128,512]{3,2,1,0:T(8,128)(2,1)S(1)} %get-tuple-element.91), channel_id=1, source_target_pairs={{0,64},{32,96},{64,0},{96,32},{128,192},{160,224},{192,128},{224,1... | collective-permute-start | bytes 1572872 | tf_op jit(solution)/shard_map/ppermute | solution.py:48
  77.9 14.9 %collective-permute-start.21 = (bf16[2,2,128,512]{3,2,1,0:T(8,128)(2,1)S(1)}, bf16[2,2,128,512]{3,2,1,0:T(8,128)(2,1)S(1)}, u32[]{:S(2)}, u32[]{:S(2)}) collective-permute-start(bf16[2,2,128,512]{3,2,1,0:T(8,128)(2,1)S(1)} %get-tuple-element.92), channel_id=1, source_target_pairs={{0,192},{32,224},{64,128},{96,160},{128,64},{160,96},{192,0},{224,... | collective-permute-start | bytes 1572872 | tf_op jit(solution)/shard_map/ppermute | solution.py:48
  80.1 14.4 %collective-permute-start.24 = (bf16[256,1024]{1,0:T(8,128)(2,1)S(1)}, bf16[256,1024]{1,0:T(8,128)(2,1)S(1)}, u32[]{:S(2)}, u32[]{:S(2)}) collective-permute-start(bf16[256,1024]{1,0:T(8,128)(2,1)S(1)} %get-tuple-element.95), channel_id=1, source_target_pairs={{0,8},{8,0},{16,24},{24,16},{1,9},{9,1},{17,25},{25,17},{2,10},{10... | collective-permute-start | bytes 1572872 | tf_op jit(solution)/shard_map/ppermute | solution.py:48
  80.1 14.4 %collective-permute-start.22 = (bf16[2,128,512]{2,1,0:T(8,128)(2,1)S(1)}, bf16[2,128,512]{2,1,0:T(8,128)(2,1)S(1)}, u32[]{:S(2)}, u32[]{:S(2)}) collective-permute-start(bf16[2,128,512]{2,1,0:T(8,128)(2,1)S(1)} %get-tuple-element.85), channel_id=1, source_target_pairs={{0,4},{1,5},{2,6},{3,7},{4,0},{5,1},{6,2},{7,3},{8,12},{9,13},{10,... | collective-permute-start | bytes 786440 | tf_op jit(solution)/shard_map/ppermute | solution.py:48
  80.1 14.4 %collective-permute-start.23 = (bf16[2,128,512]{2,1,0:T(8,128)(2,1)S(1)}, bf16[2,128,512]{2,1,0:T(8,128)(2,1)S(1)}, u32[]{:S(2)}, u32[]{:S(2)}) collective-permute-start(bf16[2,128,512]{2,1,0:T(8,128)(2,1)S(1)} %get-tuple-element.84), channel_id=1, source_target_pairs={{0,2},{1,3},{2,0},{3,1},{4,6},{5,7},{6,4},{7,5},{8,10},{9,11},{10,... | collective-permute-start | bytes 786440 | tf_op jit(solution)/shard_map/ppermute | solution.py:48
  92.8 14.5 %collective-permute-start.28 = (bf16[2,2,128,512]{3,2,1,0:T(8,128)(2,1)S(1)}, bf16[2,2,128,512]{3,2,1,0:T(8,128)(2,1)S(1)}, u32[]{:S(2)}, u32[]{:S(2)}) collective-permute-start(bf16[2,2,128,512]{3,2,1,0:T(8,128)(2,1)S(1)} %get-tuple-element.105), channel_id=1, source_target_pairs={{0,128},{32,160},{64,192},{96,224},{128,0},{160,32},{192,64},{224,... | collective-permute-start | bytes 1572872 | tf_op jit(solution)/shard_map/ppermute | solution.py:48
  94.6 12.6 %collective-permute-start.25 = (bf16[2,128,512]{2,1,0:T(8,128)(2,1)S(1)}, bf16[2,128,512]{2,1,0:T(8,128)(2,1)S(1)}, u32[]{:S(2)}, u32[]{:S(2)}) collective-permute-start(bf16[2,128,512]{2,1,0:T(8,128)(2,1)S(1)} %get-tuple-element.97), channel_id=1, source_target_pairs={{0,6},{1,7},{2,4},{3,5},{4,2},{5,3},{6,0},{7,1},{8,14},{9,15},{10,... | collective-permute-start | bytes 786440 | tf_op jit(solution)/shard_map/ppermute | solution.py:48
  96.1 24.7 %collective-permute-start.26 = (bf16[256,1024]{1,0:T(8,128)(2,1)S(1)}, bf16[256,1024]{1,0:T(8,128)(2,1)S(1)}, u32[]{:S(2)}, u32[]{:S(2)}) collective-permute-start(bf16[256,1024]{1,0:T(8,128)(2,1)S(1)} %get-tuple-element.101), channel_id=1, source_target_pairs={{0,24},{8,16},{16,8},{24,0},{1,25},{9,17},{17,9},{25,1},{2,26},{10... | collective-permute-start | bytes 1572872 | tf_op jit(solution)/shard_map/ppermute | solution.py:48
  98.2 22.6 %collective-permute-start.27 = (bf16[256,1024]{1,0:T(8,128)(2,1)S(1)}, bf16[256,1024]{1,0:T(8,128)(2,1)S(1)}, u32[]{:S(2)}, u32[]{:S(2)}) collective-permute-start(bf16[256,1024]{1,0:T(8,128)(2,1)S(1)} %get-tuple-element.102), channel_id=1, source_target_pairs={{0,16},{8,24},{16,0},{24,8},{1,17},{9,25},{17,1},{25,9},{2,18},{10... | collective-permute-start | bytes 1572872 | tf_op jit(solution)/shard_map/ppermute | solution.py:48
  107.6 17.4 %collective-permute-start.29 = (bf16[2,128,512]{2,1,0:T(8,128)(2,1)S(1)}, bf16[2,128,512]{2,1,0:T(8,128)(2,1)S(1)}, u32[]{:S(2)}, u32[]{:S(2)}) collective-permute-start(bf16[2,128,512]{2,1,0:T(8,128)(2,1)S(1)} %fusion), channel_id=1, source_target_pairs={{0,32},{32,0},{64,96},{96,64},{128,160},{160,128},{192,224},{224,1... | collective-permute-start | bytes 786440 | tf_op jit(solution)/shard_map/ppermute | solution.py:48
  (11 other events, 82.8 us)
